TPU v7x, 256 devices: a whole 4x4x8 slice. The times are simulated.
256 devices in a mesh: vec: 16 (over x, z_lo, core), pair: 16 (over z_hi, y).
Axes of the slice: x: 4, y: 4, z: 8 (z_hi: 4, z_lo: 2; z = z_hi * 2 + z_lo), core: 2. Of those that a mesh axis runs over, the one named last changes fastest.
Arguments:
- cholesky: bfloat16 [256, 1600, 1600], P('vec', 'pair'), may hold values from -0.0390625 to 0.0390625
- walkers: bfloat16 [16, 1600, 200], P('vec', 'pair'), may hold values from -1.1953125 to 1.1953125
- inv_correlation: float32 [16, 200, 200], P('vec'), may hold values from -1.25 to 1.25
- trial_orbitals: bfloat16 [1600, 200], replicated, may hold values from -0.15625 to 0.15625
- aux_fields: float32 [16, 256], P(None, 'vec'), may hold values from -4 to 4
Outputs:
- new_walkers: bfloat16 [16, 1600, 200], P('vec', 'pair')
- fields: float32 [16, 256], P(None, 'vec')
All inputs are finite; a program needn't handle non-finite values.
Results may differ from a plain program's by a relative error of at most 0.035.
Values may be sent and summed in bfloat16 or wider, within the bound.
No kernel may reach another device: no remote copies, remote signals or barrier semaphores. Data moves between devices by JAX's collectives and lax.ppermute only.
A program may use at most 64 MiB of HBM per device.

v0:
```python
import functools

import jax
import jax.numpy as jnp
from jax import lax
from jax.experimental import pallas as pl
from jax.experimental.pallas import tpu as pltpu
from jax.sharding import PartitionSpec as P

TAYLOR = 6
NX, NL, NC = 4, 2, 2
NH, NY = 4, 4
GROUP = 16

root_step = 0.5
shift_cap = 1.0

VMEM = pl.BlockSpec(memory_space=pltpu.VMEM)
SMEM = pl.BlockSpec(memory_space=pltpu.SMEM)
NT = (((1,), (1,)), ((), ()))


def vec_of(x, low, core):
    return ((x % NX) * NL + low) * NC + core


def places():
    return [(x, low, core) for x in range(NX) for low in range(NL) for core in range(NC)]


def send_x(array, step):
    return lax.ppermute(array, "vec", [(vec_of(*p), vec_of(p[0] + step, p[1], p[2])) for p in places()])


def swap_low(array):
    return lax.ppermute(array, "vec", [(vec_of(*p), vec_of(p[0], 1 - p[1], p[2])) for p in places()])


def swap_core(array):
    return lax.ppermute(array, "vec", [(vec_of(*p), vec_of(p[0], p[1], 1 - p[2])) for p in places()])


def send_y(array, step):
    return lax.ppermute(array, "pair", [(h * NY + y, h * NY + (y + step) % NY) for h in range(NH) for y in range(NY)])


def send_h(array, step):
    return lax.ppermute(array, "pair", [(h * NY + y, ((h + step) % NH) * NY + y) for h in range(NH) for y in range(NY)])


def everywhere(array, target):
    pairs = []
    for x, low, core in places():
        for high in range(NH):
            for y in range(NY):
                to = target(x, low, core, high, y)
                if to is not None:
                    pairs.append(
                        (vec_of(x, low, core) * NH * NY + high * NY + y, vec_of(*to[:3]) * NH * NY + to[3] * NY + to[4])
                    )
    return lax.ppermute(array, ("vec", "pair"), pairs)


def exchange(array):
    return everywhere(array, lambda x, low, core, high, y: (x, high // NC, high % NC, low * NC + core, y))


def first_target(x, low, core, high, y):
    turn = (high - core) % NH
    return (x, low, core if turn % 2 == 0 else 1 - core, core + 2 if turn in (0, 3) else core, y)


def second_target(x, low, core, high, y):
    turn = (high - core) % NH
    return None if turn % 2 == 0 else (x, low, 1 - core, core + 2 if turn == 1 else core, y)


def diagonal_mask(rows, columns):
    row = lax.broadcasted_iota(jnp.int32, (rows, columns), 0)
    column = lax.broadcasted_iota(jnp.int32, (rows, columns), 1)
    return (row % GROUP) == (column // GROUP)


def groups_of(rows):
    return [(start, min(GROUP, rows - start)) for start in range(0, rows, GROUP)]


def bias_kernel(r0, r1, r2, r3, own, other, out_ref):
    rows, vectors, depth = own.shape
    parts = []
    for factor in (own, other):
        total = jnp.zeros((8 * GROUP, GROUP * vectors), jnp.float32)
        tail = None
        for start, count in groups_of(rows):
            left = jnp.concatenate(
                [r[low, start : start + GROUP, :] for r in (r0, r1, r2, r3) for low in range(NL)], axis=0
            )
            right = factor[start : start + count].reshape(count * vectors, depth)
            product = lax.dot_general(left, right, NT, preferred_element_type=jnp.float32)
            if count == GROUP:
                total = total + product
            else:
                tail = product
        pieces = [total] if tail is None else [total, tail]
        summed = jnp.zeros((8, vectors), jnp.float32)
        for piece in pieces:
            width = piece.shape[1]
            kept = jnp.where(diagonal_mask(8 * GROUP, width), piece, 0.0)
            kept = jnp.sum(kept.reshape(8, GROUP, width), axis=1)
            pick = lax.broadcasted_iota(jnp.int32, (width, vectors), 0) % vectors == lax.broadcasted_iota(
                jnp.int32, (width, vectors), 1
            )
            summed = summed + jnp.dot(
                kept, pick.astype(jnp.float32), precision=lax.Precision.HIGHEST, preferred_element_type=jnp.float32
            )
        parts.append(summed)
    out_ref[...] = jnp.concatenate(parts, axis=1)


def coefficients_of(bias_refs, aux):
    b0, b1, b2, b3 = bias_refs
    bias = (b0[...] + b2[...]) + (b1[...] + b3[...])
    return aux[...] - jnp.clip(-root_step * bias, -shift_cap, shift_cap)


def block_diagonals(coefficients, vectors):
    tall, wide = 8 * GROUP, GROUP * vectors
    spread = (
        lax.broadcasted_iota(jnp.int32, (tall, 8), 0) // GROUP == lax.broadcasted_iota(jnp.int32, (tall, 8), 1)
    ).astype(jnp.bfloat16)
    repeat = (
        lax.broadcasted_iota(jnp.int32, (vectors, wide), 1) % vectors
        == lax.broadcasted_iota(jnp.int32, (vectors, wide), 0)
    ).astype(jnp.bfloat16)
    mask = diagonal_mask(tall, wide)
    blocks = []
    for at in range(2):
        piece = coefficients[:, at * vectors : (at + 1) * vectors]
        piece = jnp.dot(spread, piece, preferred_element_type=jnp.float32).astype(jnp.bfloat16)
        piece = jnp.dot(piece, repeat, preferred_element_type=jnp.float32)
        blocks.append(jnp.where(mask, piece, 0.0).astype(jnp.bfloat16))
    return blocks


def walker_sums(blocks, own, other, base, half, walkers, store):
    vectors, columns = own.shape[1:]
    for start, count in groups_of(half):
        depth = count * vectors
        lefts = [
            jnp.concatenate([block[w * GROUP : (w + 1) * GROUP, :depth] for w in walkers], axis=0) for block in blocks
        ]
        for left in range(0, columns, 512):
            right = min(columns, left + 512)
            total = 0.0
            for block, source in zip(lefts, (own, other)):
                total = total + jnp.dot(
                    block,
                    source[pl.ds(base + start, count), :, left:right].reshape(depth, right - left),
                    preferred_element_type=jnp.float32,
                )
            total = total.astype(jnp.bfloat16)
            for at, walker in enumerate(walkers):
                store(walker, start, count, left, right, total[at * GROUP : at * GROUP + count, :])


ODD = [step * NL + 1 for step in range(NX)]
EVEN = [step * NL for step in range(NX)]


def send_kernel(at, b0, b1, b2, b3, aux, own, other, fields_ref, send_ref):
    half = own.shape[0] // NL
    fields = coefficients_of((b0, b1, b2, b3), aux)
    fields_ref[...] = fields
    blocks = block_diagonals((root_step * fields).astype(jnp.bfloat16), own.shape[1])

    def store(walker, start, count, left, right, value):
        send_ref[walker // NL, start : start + count, left:right] = value

    walker_sums(blocks, own, other, (1 - at[0]) * half, half, ODD, store)


def keep_kernel(at, fields, own, other, p0, p1, p2, p3, keep_ref):
    half = own.shape[0] // NL
    blocks = block_diagonals((root_step * fields[...]).astype(jnp.bfloat16), own.shape[1])
    outs = (p0, p1, p2, p3)

    def store_even(side):
        def store(walker, start, count, left, right, value):
            outs[walker // NL][side, start : start + count, left:right] = value

        return store

    def store_all(walker, start, count, left, right, value):
        if walker % NL == 0:
            outs[walker // NL][0, start : start + count, left:right] = value
        else:
            keep_ref[walker // NL, start : start + count, left:right] = value

    walker_sums(blocks, own, other, (1 - at[0]) * half, half, EVEN, store_even(1))
    walker_sums(blocks, own, other, at[0] * half, half, EVEN + ODD, store_all)


def wide(value):
    return value.astype(jnp.float32)


def pair_sum_kernel(keep, arrived, o0, o1, o2, o3):
    for step, out in enumerate((o0, o1, o2, o3)):
        out[...] = (wide(keep[step]) + wide(arrived[step])).astype(out.dtype)


def x_sum_kernel(p0, p1, p2, p3, out):
    out[...] = ((wide(p0[1]) + wide(p1[1])) + (wide(p2[1]) + wide(p3[1]))).astype(out.dtype)


def last_sum_kernel(at, p0, p1, p2, p3, arrived, q0, q1, q2, q3, first, second):
    even = ((wide(p0[0]) + wide(p1[0])) + (wide(p2[0]) + wide(p3[0]))) + wide(arrived[...])
    odd = (wide(q0[...]) + wide(q1[...])) + (wide(q2[...]) + wide(q3[...]))
    turn = (at[0] - at[1] + NH) % NH
    pick = jnp.logical_or(turn == 1, turn == 2)
    first[...] = jnp.where(pick, even, odd).astype(first.dtype)
    second[...] = jnp.where(pick, odd, even).astype(second.dtype)


def stack_kernel(*refs):
    for step, ref in enumerate(refs[:-1]):
        refs[-1][step] = ref[...]


def taylor_kernel(at, *refs):
    pieces, (w0, w1, w2, w3), (out_ref, held, operator, terms, total) = refs[:12], refs[12:16], refs[16:]
    high, y, low, core = at[0], at[1], at[2], at[3]
    half = held.shape[1]
    rows = 2 * half
    for side in range(2):
        base = high + (((high % 2) ^ core ^ side) & 1)
        mine = pieces[side * 6 : side * 6 + 6]
        for step in range(NY):
            row = ((base % NH) * NY + (y - step + NY) % NY) * NL
            held[row + low] = mine[step][0]
            held[row + 1 - low] = mine[step][1]
            row = (((base + 2) % NH) * NY + (y - step + NY) % NY) * NL
            held[row + low] = mine[4][step]
            held[row + 1 - low] = mine[5][step]
    for block in range(NH * NY * NL):
        operator[block * half : (block + 1) * half, :] = held[block]
    spread = terms.shape[2]
    for step, ref in enumerate((w0, w1, w2, w3)):
        total[step] = ref[...]
    for block in range(NH * NY):
        piece = total[
            (y - block % NY + NY) % NY, (((block // NY // NC) ^ low) * NC + ((block // NY % NC) ^ core))
        ]
        terms[0, block * rows : (block + 1) * rows, :] = piece
    chunk = 400
    mine = low * NC + core

    def one_term(degree, accumulated):
        source = (degree - 1) % 2

        @pl.loop(0, operator.shape[0] // chunk)
        def _(index):
            place = pl.ds(pl.multiple_of(index * chunk, 16), chunk)
            product = jnp.dot(operator[place, :], terms[source], preferred_element_type=jnp.float32)
            terms[1 - source, place, :] = (product / degree.astype(jnp.float32)).astype(jnp.bfloat16)

        picked = jnp.zeros((rows, spread), jnp.float32)
        for block in range(NH * NY):
            piece = wide(terms[1 - source, block * rows : (block + 1) * rows, :])
            picked = jnp.where(mine * NY + y == block, piece, picked)
        return accumulated + picked

    accumulated = lax.fori_loop(1, TAYLOR + 1, one_term, wide(w0[0]))
    out_ref[...] = accumulated.astype(out_ref.dtype)


def call(kernel, outs, args, name, scratch=(), smem=0):
    return pl.pallas_call(
        kernel,
        out_shape=outs,
        in_specs=[SMEM] * smem + [VMEM] * (len(args) - smem),
        out_specs=[VMEM] * len(outs) if isinstance(outs, (list, tuple)) else VMEM,
        scratch_shapes=list(scratch),
        compiler_params=pltpu.CompilerParams(vmem_limit_bytes=48 * 2**20),
        name=name,
    )(*args)


def on_device(cholesky, walkers, inv_correlation, trial_orbitals, aux_fields):
    vectors, rows, orbitals = cholesky.shape
    occupied = walkers.shape[2]
    half = rows // NL
    bf16 = jnp.bfloat16
    me = lax.axis_index("vec")
    x, low, core = me // (NL * NC), (me // NC) % NL, me % NC
    pair = lax.axis_index("pair")
    high, y = pair // NY, pair % NY

    own = jnp.transpose(cholesky, (1, 0, 2))
    other = swap_core(own)
    aux_other = swap_core(aux_fields)

    rotated = jnp.dot(
        walkers[0].astype(jnp.float32), inv_correlation[0], precision=lax.Precision.HIGHEST
    ).astype(bf16)
    rotated = jnp.pad(rotated, ((0, -rows % GROUP), (0, 0)))
    partner = swap_low(rotated)
    both = jnp.where(low == 0, jnp.stack([rotated, partner]), jnp.stack([partner, rotated]))
    met = [both] + [send_x(both, -step) for step in range(1, NX)]

    factor = jnp.einsum("pgq,qm->pgm", own, trial_orbitals, preferred_element_type=jnp.float32).astype(bf16)
    bias = call(
        bias_kernel,
        jax.ShapeDtypeStruct((8, 2 * vectors), jnp.float32),
        (*met, factor, swap_core(factor)),
        "force_bias",
    )
    from_y = [bias] + [send_y(bias, step) for step in range(1, NY)]
    bias = (from_y[0] + from_y[2]) + (from_y[1] + from_y[3])
    from_h = [bias] + [send_h(bias, step) for step in range(1, NH)]

    order = jnp.arange(NX * NL)
    mine = vec_of(x + order // NL, order % NL, core)
    aux = jnp.concatenate([jnp.take(aux_fields, mine, axis=0), jnp.take(aux_other, mine, axis=0)], axis=1)

    piece = jax.ShapeDtypeStruct((half, orbitals), bf16)
    quad = jax.ShapeDtypeStruct((NX, half, orbitals), bf16)
    two = jax.ShapeDtypeStruct((2, half, orbitals), bf16)
    where = low.reshape(1).astype(jnp.int32)
    shifted, away = call(
        send_kernel,
        [jax.ShapeDtypeStruct((8, 2 * vectors), jnp.float32), quad],
        (where, *from_h, aux, own, other),
        "operator_away",
        smem=1,
    )
    away = swap_low(away)
    *parts, keep = call(keep_kernel, [two] * NX + [quad], (where, shifted, own, other), "operator_keep", smem=1)
    parts = [parts[0]] + [send_x(parts[step], step) for step in range(1, NX)]
    odd = call(pair_sum_kernel, [piece] * NX, (keep, away), "pair_sum")
    odd = [odd[0]] + [send_x(odd[step], step) for step in range(1, NX)]
    even = swap_low(call(x_sum_kernel, piece, tuple(parts), "x_sum"))
    turn = jnp.stack([high, core]).astype(jnp.int32)
    first, second = call(last_sum_kernel, [piece] * 2, (turn, *parts, even, *odd), "last_sum", smem=1)

    both = jnp.concatenate([shifted[:, :vectors], swap_core(shifted[:, vectors:])])
    walker = jnp.arange(NX * NL * NC)
    place = (
        ((walker % NC) ^ core) * (NX * NL) + ((walker // (NL * NC) - x) % NX) * NL + ((walker // NC) % NL)
    )
    fields = jnp.take(both, place, axis=0)

    late, _ = lax.optimization_barrier((walkers[0], shifted))
    rows_here = exchange(late)
    two_rows = jnp.stack([rows_here, swap_core(rows_here)])
    four_rows = jnp.concatenate([two_rows, swap_low(two_rows)])
    all_rows = [four_rows] + [send_y(four_rows, step) for step in range(1, NY)]

    active = (high + core) % 2 == 0
    got = everywhere(first, first_target)
    more = everywhere(second, second_target)
    block0 = jnp.where(active, second, got)
    block1 = jnp.where(active, got, more)
    low0 = swap_low(block0)
    quad1 = call(stack_kernel, quad, (block1, *[send_y(block1, step) for step in range(1, NY)]), "stack_y")
    pair0 = call(stack_kernel, two, (block0, low0), "stack_low")
    pieces = [pair0] + [send_y(pair0, step) for step in range(1, NY)] + [quad1, swap_low(quad1)]
    pieces = pieces + [swap_core(p) for p in pieces]
    position = jnp.stack([high, y, low, core]).astype(jnp.int32)
    updated = call(
        taylor_kernel,
        jax.ShapeDtypeStruct((rows, occupied), bf16),
        (position, *pieces, *all_rows),
        "taylor",
        scratch=[
            pltpu.VMEM((NH * NY * NL, half, orbitals), bf16),
            pltpu.VMEM((orbitals, orbitals), bf16),
            pltpu.VMEM((2, orbitals, occupied), bf16),
            pltpu.VMEM((NY, 4, rows, occupied), bf16),
        ],
        smem=1,
    )
    return (exchange(updated)[None], fields)


def solution(mesh):
    placed = (
        P("vec", "pair", None),
        P("vec", "pair", None),
        P("vec", None, None),
        P(),
        P(None, "vec"),
    )
    return jax.shard_map(
        on_device,
        mesh=mesh,
        in_specs=placed,
        out_specs=(P("vec", "pair", None), P(None, "vec")),
        check_vma=False,
    )
```

profile of v0, /device:TPU:33, one launch (start us, length us, event | category | flops | bytes accessed | tf_op | source)
XLA Modules:
  0.0 210.2 jit_solution(17798534944654042446)
XLA Ops:
  0.7 0.8 collective-permute-start.12
  1.7 4.2 %convolution_convert_fusion.own = bf16[100,16,200]{2,1,0:T(8,128)(2,1)S(1)} fusion(bf16[1600,200]{0,1:T(8,128)(2,1)S(1)} %copy-done, bf16[16,100,1600]{2,0,1:T(8,128)(2,1)} %param.7), kind=kOutput, calls=%fused_computation.3 | convolution fusion | flops 1024320000 | bytes 6400000 | tf_op jit(solution)/shard_map/pgq,qm->pgm/dot_general | solution.py:311
  5.9 0.8 collective-permute-start.4
  7.2 1.7 collective-permute-start
  9.2 1.8 collective-permute-done
  11.1 2.3 %collective-permute-start.1 = (bf16[2,112,200]{2,1,0:T(8,128)(2,1)S(1)}, bf16[2,112,200]{2,1,0:T(8,128)(2,1)S(1)}, u32[]{:S(2)}, u32[]{:S(2)}) collective-permute-start(bf16[2,112,200]{2,1,0:T(8,128)(2,1)S(1)} %maximum_select_fusion.r0), channel_id=1, source_target_pairs={{0,192},{16,208},{32,224},{48,240},{64,0},{80,16},{96,32},{112,48}... | collective-permute-start | bytes 268808 | tf_op jit(solution)/shard_map/ppermute | solution.py:32
  15.7 3.0 %collective-permute-done.2.r2 = bf16[2,112,200]{2,1,0:T(8,128)(2,1)S(1)} collective-permute-done((bf16[2,112,200]{2,1,0:T(8,128)(2,1)S(1)}, bf16[2,112,200]{2,1,0:T(8,128)(2,1)S(1)}, u32[]{:S(2)}, u32[]{:S(2)}) %collective-permute-start.2) | collective-permute-done | bytes 89632 | tf_op jit(solution)/shard_map/ppermute | solution.py:32
  18.7 3.2 %collective-permute-done.3.r3 = bf16[2,112,200]{2,1,0:T(8,128)(2,1)S(1)} collective-permute-done((bf16[2,112,200]{2,1,0:T(8,128)(2,1)S(1)}, bf16[2,112,200]{2,1,0:T(8,128)(2,1)S(1)}, u32[]{:S(2)}, u32[]{:S(2)}) %collective-permute-start.3) | collective-permute-done | bytes 89632 | tf_op jit(solution)/shard_map/ppermute | solution.py:32
  21.9 1.5 force_bias.1
  23.4 1.3 collective-permute-start.6
  24.7 1.5 collective-permute-start.7
  26.2 1.6 collective-permute-start.5
  27.9 2.3 %collective-permute-done.5 = f32[8,32]{1,0:T(8,128)S(1)} collective-permute-done((f32[8,32]{1,0:T(8,128)S(1)}, f32[8,32]{1,0:T(8,128)S(1)}, u32[]{:S(2)}, u32[]{:S(2)}) %collective-permute-start.5) | collective-permute-done | bytes 1056 | tf_op jit(solution)/shard_map/ppermute | solution.py:44
  30.2 3.0 %collective-permute-start.8 = (f32[8,32]{1,0:T(8,128)S(1)}, f32[8,32]{1,0:T(8,128)S(1)}, u32[]{:S(2)}, u32[]{:S(2)}) collective-permute-start(f32[8,32]{1,0:T(8,128)S(1)} %add_add_fusion.b0), channel_id=1, source_target_pairs={{0,4},{1,5},{2,6},{3,7},{4,8},{5,9},{6,10},{7,11},{8,12},{9,13},{1... | collective-permute-start | bytes 3080 | tf_op jit(solution)/shard_map/ppermute | solution.py:48
  33.1 4.2 %collective-permute-start.9 = (f32[8,32]{1,0:T(8,128)S(1)}, f32[8,32]{1,0:T(8,128)S(1)}, u32[]{:S(2)}, u32[]{:S(2)}) collective-permute-start(f32[8,32]{1,0:T(8,128)S(1)} %add_add_fusion.b0), channel_id=1, source_target_pairs={{0,8},{1,9},{2,10},{3,11},{4,12},{5,13},{6,14},{7,15},{8,0},{9,1},... | collective-permute-start | bytes 3080 | tf_op jit(solution)/shard_map/ppermute | solution.py:48
  37.3 2.4 %collective-permute-start.10 = (f32[8,32]{1,0:T(8,128)S(1)}, f32[8,32]{1,0:T(8,128)S(1)}, u32[]{:S(2)}, u32[]{:S(2)}) collective-permute-start(f32[8,32]{1,0:T(8,128)S(1)} %add_add_fusion.b0), channel_id=1, source_target_pairs={{0,12},{1,13},{2,14},{3,15},{4,0},{5,1},{6,2},{7,3},{8,4},{9,5},{1... | collective-permute-start | bytes 3080 | tf_op jit(solution)/shard_map/ppermute | solution.py:48
  39.8 0.9 collective-permute-done.10.b3
  40.7 2.5 %copy-done.1 = bf16[16,100,1600]{2,0,1:T(8,128)(2,1)S(1)} copy-done((bf16[16,100,1600]{2,0,1:T(8,128)(2,1)S(1)}, bf16[16,100,1600]{2,0,1:T(8,128)(2,1)}, u32[]{:S(2)}) %copy-start.1) | copy-done | bytes 5120024
  43.2 3.9 %operator_away.1 = (f32[8,32]{1,0:T(8,128)S(1)}, bf16[4,50,1600]{2,1,0:T(8,128)(2,1)S(1)}) custom-call(s32[1]{0:T(128)} %bitcast.2.at, f32[8,32]{1,0:T(8,128)S(1)} %add_add_fusion.b0, f32[8,32]{1,0:T(8,128)S(1)} %collective-permute-done.8.b1, f32[8,32]{1,0:T(8,128)S(1)} %collective-permute-done.9.b2, f32[8,32]{1,0:T(8,128)S(1)} %collective-permute-done.10.b3, ...), custom_call_target="tpu_custom_call" | custom-call | tf_op jit(solution)/shard_map/operator_away/pallas_call | solution.py:278
  47.4 0.9 collective-permute-start.17
  48.2 6.5 %operator_keep.1 = (bf16[2,50,1600]{2,1,0:T(8,128)(2,1)S(1)}, bf16[2,50,1600]{2,1,0:T(8,128)(2,1)S(1)}, bf16[2,50,1600]{2,1,0:T(8,128)(2,1)S(1)}, bf16[2,50,1600...) custom-call(s32[1]{0:T(128)} %bitcast.2.at, f32[8,32]{1,0:T(8,128)S(1)} %get-tuple-element.17.fields, ...), custom_call_target="tpu_custom_call" | custom-call | tf_op jit(solution)/shard_map/operator_keep/pallas_call | solution.py:278
  55.3 2.2 %collective-permute-start.15 = (bf16[2,50,1600]{2,1,0:T(8,128)(2,1)S(1)}, bf16[2,50,1600]{2,1,0:T(8,128)(2,1)S(1)}, u32[]{:S(2)}, u32[]{:S(2)}) collective-permute-start(bf16[2,50,1600]{2,1,0:T(8,128)(2,1)S(1)} %get-tuple-element.21), channel_id=1, source_target_pairs={{0,192},{16,208},{32,224},{48,240},{64,0},{80,16},{96,32},{112,48}... | collective-permute-start | bytes 960008 | tf_op jit(solution)/shard_map/ppermute | solution.py:32
  57.5 10.7 %collective-permute-done.13.p1 = bf16[2,50,1600]{2,1,0:T(8,128)(2,1)S(1)} collective-permute-done((bf16[2,50,1600]{2,1,0:T(8,128)(2,1)S(1)}, bf16[2,50,1600]{2,1,0:T(8,128)(2,1)S(1)}, u32[]{:S(2)}, u32[]{:S(2)}) %collective-permute-start.13) | collective-permute-done | bytes 320032 | tf_op jit(solution)/shard_map/ppermute | solution.py:32
  68.2 4.1 %collective-permute-done.15.p3 = bf16[2,50,1600]{2,1,0:T(8,128)(2,1)S(1)} collective-permute-done((bf16[2,50,1600]{2,1,0:T(8,128)(2,1)S(1)}, bf16[2,50,1600]{2,1,0:T(8,128)(2,1)S(1)}, u32[]{:S(2)}, u32[]{:S(2)}) %collective-permute-start.15) | collective-permute-done | bytes 320032 | tf_op jit(solution)/shard_map/ppermute | solution.py:32
  73.3 0.8 pair_sum.1
  74.7 4.0 %collective-permute-start.19 = (bf16[50,1600]{1,0:T(8,128)(2,1)}, bf16[50,1600]{1,0:T(8,128)(2,1)S(1)}, u32[]{:S(2)}, u32[]{:S(2)}) collective-permute-start(bf16[50,1600]{1,0:T(8,128)(2,1)} %get-tuple-element.26), channel_id=1, source_target_pairs={{0,128},{16,144},{32,160},{48,176},{64,192},{80,208},{96,224},{112... | collective-permute-start | bytes 480008 | tf_op jit(solution)/shard_map/ppermute | solution.py:32
  78.8 1.9 collective-permute-done.18.q1
  80.6 4.3 %collective-permute-done.19.q2 = bf16[50,1600]{1,0:T(8,128)(2,1)S(1)} collective-permute-done((bf16[50,1600]{1,0:T(8,128)(2,1)}, bf16[50,1600]{1,0:T(8,128)(2,1)S(1)}, u32[]{:S(2)}, u32[]{:S(2)}) %collective-permute-start.19) | collective-permute-done | bytes 160032 | tf_op jit(solution)/shard_map/ppermute | solution.py:32
  84.9 0.8 last_sum.1
  85.7 7.7 %collective-permute-start.21 = (bf16[50,1600]{1,0:T(8,128)(2,1)S(1)}, bf16[50,1600]{1,0:T(8,128)(2,1)S(1)}, u32[]{:S(2)}, u32[]{:S(2)}) collective-permute-start(bf16[50,1600]{1,0:T(8,128)(2,1)S(1)} %get-tuple-element.29), channel_id=1, source_target_pairs={{0,8},{1,9},{2,10},{3,11},{4,16},{5,17},{6,18},{7,19},{8,0},{9,1},... | collective-permute-start | bytes 480008 | tf_op jit(solution)/shard_map/ppermute | solution.py:61
  93.4 1.9 collective-permute-start.26
  95.4 5.3 %collective-permute-done.21 = bf16[50,1600]{1,0:T(8,128)(2,1)S(1)} collective-permute-done((bf16[50,1600]{1,0:T(8,128)(2,1)S(1)}, bf16[50,1600]{1,0:T(8,128)(2,1)S(1)}, u32[]{:S(2)}, u32[]{:S(2)}) %collective-permute-start.21) | collective-permute-done | bytes 160032 | tf_op jit(solution)/shard_map/ppermute | solution.py:61
  100.7 3.7 %collective-permute-done.26 = bf16[50,1600]{1,0:T(8,128)(2,1)S(1)} collective-permute-done((bf16[50,1600]{1,0:T(8,128)(2,1)S(1)}, bf16[50,1600]{1,0:T(8,128)(2,1)S(1)}, u32[]{:S(2)}, u32[]{:S(2)}) %collective-permute-start.26) | collective-permute-done | bytes 160032 | tf_op jit(solution)/shard_map/ppermute | solution.py:61
  104.6 2.5 %collective-permute-start.28 = (bf16[50,1600]{1,0:T(8,128)(2,1)S(1)}, bf16[50,1600]{1,0:T(8,128)(2,1)S(1)}, u32[]{:S(2)}, u32[]{:S(2)}) collective-permute-start(bf16[50,1600]{1,0:T(8,128)(2,1)S(1)} %get-tuple-element.39.refs_0_), channel_id=1, source_target_pairs={{0,2},{1,3},{2,0},{3,1},{4,6},{5,7},{6,4},{7,5},{8,10},{9,11},{10,... | collective-permute-start | bytes 480008 | tf_op jit(solution)/shard_map/ppermute | solution.py:44
  107.1 1.0 collective-permute-start.29
  108.1 7.3 %collective-permute-done.27.refs_1_ = bf16[50,1600]{1,0:T(8,128)(2,1)S(1)} collective-permute-done((bf16[50,1600]{1,0:T(8,128)(2,1)S(1)}, bf16[50,1600]{1,0:T(8,128)(2,1)S(1)}, u32[]{:S(2)}, u32[]{:S(2)}) %collective-permute-start.27) | collective-permute-done | bytes 160032 | tf_op jit(solution)/shard_map/ppermute | solution.py:44
  115.4 0.9 collective-permute-done.29.refs_3_
  116.4 1.1 copy.24
  117.7 2.2 %collective-permute-start.37 = (bf16[100,200]{1,0:T(8,128)(2,1)S(1)}, bf16[100,200]{1,0:T(8,128)(2,1)S(1)}, u32[]{:S(2)}, u32[]{:S(2)}) collective-permute-start(bf16[100,200]{1,0:T(8,128)(2,1)S(1)} %bitcast.34), channel_id=1, source_target_pairs={{0,0},{1,1},{2,2},{3,3},{4,16},{5,17},{6,18},{7,19},{8,32},{9,33},... | collective-permute-start | bytes 120008 | tf_op jit(solution)/shard_map/ppermute | solution.py:61
  119.9 13.8 %collective-permute-done.37 = bf16[100,200]{1,0:T(8,128)(2,1)S(1)} collective-permute-done((bf16[100,200]{1,0:T(8,128)(2,1)S(1)}, bf16[100,200]{1,0:T(8,128)(2,1)S(1)}, u32[]{:S(2)}, u32[]{:S(2)}) %collective-permute-start.37) | collective-permute-done | bytes 40032 | tf_op jit(solution)/shard_map/ppermute | solution.py:61
  133.7 1.2 collective-permute-done.38
  135.0 1.3 collective-permute-start.39
  136.7 2.8 %collective-permute-done.39 = bf16[2,100,200]{2,1,0:T(8,128)(2,1)S(1)} collective-permute-done((bf16[2,100,200]{2,1,0:T(8,128)(2,1)S(1)}, bf16[2,100,200]{2,1,0:T(8,128)(2,1)S(1)}, u32[]{:S(2)}, u32[]{:S(2)}) %collective-permute-start.39) | collective-permute-done | bytes 80032 | tf_op jit(solution)/shard_map/ppermute | solution.py:36
  139.6 1.1 collective-permute-start.40
  140.7 2.5 %collective-permute-start.41 = (bf16[4,100,200]{2,1,0:T(8,128)(2,1)S(1)}, bf16[4,100,200]{2,1,0:T(8,128)(2,1)S(1)}, u32[]{:S(2)}, u32[]{:S(2)}) collective-permute-start(bf16[4,100,200]{2,1,0:T(8,128)(2,1)S(1)} %pad_maximum_fusion.refs_12_), channel_id=1, source_target_pairs={{0,2},{1,3},{2,0},{3,1},{4,6},{5,7},{6,4},{7,5},{8,10},{9,11},{10,... | collective-permute-start | bytes 480008 | tf_op jit(solution)/shard_map/ppermute | solution.py:44
  143.1 1.3 collective-permute-start.22
  144.5 1.8 collective-permute-start.36
  146.4 1.5 collective-permute-done.22.refs_1_
  147.8 2.4 %collective-permute-start.44 = (f32[8,16]{1,0:T(8,128)S(1)}, f32[8,16]{1,0:T(8,128)S(1)}, u32[]{:S(2)}, u32[]{:S(2)}) collective-permute-start(f32[8,16]{1,0:T(8,128)S(1)} %get-tuple-element.44), channel_id=1, source_target_pairs={{0,16},{16,0},{32,48},{48,32},{64,80},{80,64},{96,112},{112,96},{1... | collective-permute-start | bytes 1544 | tf_op jit(solution)/shard_map/ppermute | solution.py:40
  150.3 0.8 collective-permute-done.44
  151.8 1.5 collective-permute-start.24
  153.9 1.2 collective-permute-start.25
  155.2 15.0 %collective-permute-done.23.refs_1_ = bf16[2,50,1600]{2,1,0:T(8,128)(2,1)S(1)} collective-permute-done((bf16[2,50,1600]{2,1,0:T(8,128)(2,1)S(1)}, bf16[2,50,1600]{2,1,0:T(8,128)(2,1)S(1)}, u32[]{:S(2)}, u32[]{:S(2)}) %collective-permute-start.23) | collective-permute-done | bytes 320032 | tf_op jit(solution)/shard_map/ppermute | solution.py:44
  170.2 1.2 collective-permute-start.31
  171.4 1.3 collective-permute-start.33
  172.7 2.7 %collective-permute-start.42 = (bf16[4,100,200]{2,1,0:T(8,128)(2,1)S(1)}, bf16[4,100,200]{2,1,0:T(8,128)(2,1)}, u32[]{:S(2)}, u32[]{:S(2)}) collective-permute-start(bf16[4,100,200]{2,1,0:T(8,128)(2,1)S(1)} %pad_maximum_fusion.refs_12_), channel_id=1, source_target_pairs={{0,3},{1,0},{2,1},{3,2},{4,7},{5,4},{6,5},{7,6},{8,11},{9,8},{10,9... | collective-permute-start | bytes 480008 | tf_op jit(solution)/shard_map/ppermute | solution.py:44
  176.0 1.2 copy.26.refs_5_
  177.2 1.2 copy.27.refs_10_
  178.4 2.1 copy.28.refs_11_
  180.5 0.9 copy-done.3
  181.4 0.9 copy-done.5
  182.4 17.5 %taylor.1 = bf16[100,200]{1,0:T(8,128)(2,1)S(1)} custom-call(s32[4]{0:T(128)S(1)} %pad_add_fusion.at, bf16[2,50,1600]{2,1,0:T(8,128)(2,1)S(1)} %stack_low.1.refs_0_, bf16[2,50,1600]{2,1,0:T(8,128)(2,1)S(1)} %collective-permute-done.23.refs_1_, bf16[2,50,1600]{2,1,0:T(8,128)(2,1)S(1)} %collective-permute-done.24.refs_2_, ...), custom_call_target="tpu_custom_call" | custom-call | tf_op jit(solution)/shard_map/taylor/pallas_call | solution.py:278
  199.8 7.8 %collective-permute-start.43 = (bf16[100,200]{1,0:T(8,128)(2,1)S(1)}, bf16[100,200]{1,0:T(8,128)(2,1)S(1)}, u32[]{:S(2)}, u32[]{:S(2)}) collective-permute-start(bf16[100,200]{1,0:T(8,128)(2,1)S(1)} %taylor.1), channel_id=1, source_target_pairs={{0,0},{1,1},{2,2},{3,3},{4,16},{5,17},{6,18},{7,19},{8,32},{9,33},... | collective-permute-start | bytes 120008 | tf_op jit(solution)/shard_map/ppermute | solution.py:61
  208.3 1.1 collective-permute-done.43
  (85 shorter events, 10.6 us)
Async XLA Ops:
  0.6 1.1 copy-start
  0.6 6.0 %copy-start.7 = (f32[1,200,200]{2,1,0:T(8,128)S(1)}, f32[1,200,200]{2,1,0:T(8,128)}, u32[]{:S(2)}) copy-start(f32[1,200,200]{2,1,0:T(8,128)} %param.9) | copy-start | bytes 480004
  0.7 6.0 %copy-start.6 = (bf16[1,100,200]{1,2,0:T(8,128)(2,1)S(1)}, bf16[1,100,200]{1,2,0:T(8,128)(2,1)}, u32[]{:S(2)}) copy-start(bf16[1,100,200]{1,2,0:T(8,128)(2,1)} %param.8) | copy-start | bytes 120004
  0.7 8.2 %copy-start.8 = (f32[16,16]{1,0:T(8,128)S(1)}, f32[16,16]{1,0:T(8,128)}, u32[]{:S(2)}) copy-start(f32[16,16]{1,0:T(8,128)} %param.11) | copy-start | bytes 3076
  0.7 40.0 %collective-permute-start.12 = (bf16[100,16,1600]{2,1,0:T(8,128)(2,1)}, bf16[100,16,1600]{2,1,0:T(8,128)(2,1)}, u32[]{:S(2)}, u32[]{:S(2)}) collective-permute-start(bf16[100,16,1600]{2,1,0:T(8,128)(2,1)} %bitcast.25), channel_id=1, source_target_pairs={{0,16},{16,0},{32,48},{48,32},{64,80},{80,64},{96,112},{112,96},{1... | collective-permute-start | bytes 15360008 | tf_op jit(solution)/shard_map/ppermute | solution.py:40
  5.9 15.9 %collective-permute-start.4 = (bf16[100,16,200]{2,1,0:T(8,128)(2,1)S(1)}, bf16[100,16,200]{2,1,0:T(8,128)(2,1)S(1)}, u32[]{:S(2)}, u32[]{:S(2)}) collective-permute-start(bf16[100,16,200]{2,1,0:T(8,128)(2,1)S(1)} %convolution_convert_fusion.own), channel_id=1, source_target_pairs={{0,16},{16,0},{32,48},{48,32},{64,80},{80,64},{96,112},{112,96},{1... | collective-permute-start | bytes 1920008 | tf_op jit(solution)/shard_map/ppermute | solution.py:40
  7.2 3.8 %collective-permute-start = (bf16[112,200]{1,0:T(8,128)(2,1)S(1)}, bf16[112,200]{1,0:T(8,128)(2,1)S(1)}, u32[]{:S(2)}, u32[]{:S(2)}) collective-permute-start(bf16[112,200]{1,0:T(8,128)(2,1)S(1)} %get-tuple-element.42), channel_id=1, source_target_pairs={{0,32},{16,48},{32,0},{48,16},{64,96},{80,112},{96,64},{112,80},{1... | collective-permute-start | bytes 134408 | tf_op jit(solution)/shard_map/ppermute | solution.py:36
  8.9 5.1 %collective-permute-start.11 = (f32[16,16]{1,0:T(8,128)S(1)}, f32[16,16]{1,0:T(8,128)S(1)}, u32[]{:S(2)}, u32[]{:S(2)}) collective-permute-start(f32[16,16]{1,0:T(8,128)S(1)} %copy-done.8), channel_id=1, source_target_pairs={{0,16},{16,0},{32,48},{48,32},{64,80},{80,64},{96,112},{112,96},{1... | collective-permute-start | bytes 3080 | tf_op jit(solution)/shard_map/ppermute | solution.py:40
  11.1 4.6 %collective-permute-start.1 = (bf16[2,112,200]{2,1,0:T(8,128)(2,1)S(1)}, bf16[2,112,200]{2,1,0:T(8,128)(2,1)S(1)}, u32[]{:S(2)}, u32[]{:S(2)}) collective-permute-start(bf16[2,112,200]{2,1,0:T(8,128)(2,1)S(1)} %maximum_select_fusion.r0), channel_id=1, source_target_pairs={{0,192},{16,208},{32,224},{48,240},{64,0},{80,16},{96,32},{112,48}... | collective-permute-start | bytes 268808 | tf_op jit(solution)/shard_map/ppermute | solution.py:32
  13.4 5.3 %collective-permute-start.2 = (bf16[2,112,200]{2,1,0:T(8,128)(2,1)S(1)}, bf16[2,112,200]{2,1,0:T(8,128)(2,1)S(1)}, u32[]{:S(2)}, u32[]{:S(2)}) collective-permute-start(bf16[2,112,200]{2,1,0:T(8,128)(2,1)S(1)} %maximum_select_fusion.r0), channel_id=1, source_target_pairs={{0,128},{16,144},{32,160},{48,176},{64,192},{80,208},{96,224},{112... | collective-permute-start | bytes 268808 | tf_op jit(solution)/shard_map/ppermute | solution.py:32
  13.9 7.9 %collective-permute-start.3 = (bf16[2,112,200]{2,1,0:T(8,128)(2,1)S(1)}, bf16[2,112,200]{2,1,0:T(8,128)(2,1)S(1)}, u32[]{:S(2)}, u32[]{:S(2)}) collective-permute-start(bf16[2,112,200]{2,1,0:T(8,128)(2,1)S(1)} %maximum_select_fusion.r0), channel_id=1, source_target_pairs={{0,64},{16,80},{32,96},{48,112},{64,128},{80,144},{96,160},{112,17... | collective-permute-start | bytes 268808 | tf_op jit(solution)/shard_map/ppermute | solution.py:32
  23.4 4.5 %collective-permute-start.6 = (f32[8,32]{1,0:T(8,128)S(1)}, f32[8,32]{1,0:T(8,128)S(1)}, u32[]{:S(2)}, u32[]{:S(2)}) collective-permute-start(f32[8,32]{1,0:T(8,128)S(1)} %force_bias.1), channel_id=1, source_target_pairs={{0,1},{1,2},{2,3},{3,0},{4,5},{5,6},{6,7},{7,4},{8,9},{9,10},{10,1... | collective-permute-start | bytes 3080 | tf_op jit(solution)/shard_map/ppermute | solution.py:44
  24.7 3.2 %collective-permute-start.7 = (f32[8,32]{1,0:T(8,128)S(1)}, f32[8,32]{1,0:T(8,128)S(1)}, u32[]{:S(2)}, u32[]{:S(2)}) collective-permute-start(f32[8,32]{1,0:T(8,128)S(1)} %force_bias.1), channel_id=1, source_target_pairs={{0,3},{1,0},{2,1},{3,2},{4,7},{5,4},{6,5},{7,6},{8,11},{9,8},{10,9... | collective-permute-start | bytes 3080 | tf_op jit(solution)/shard_map/ppermute | solution.py:44
  26.2 4.0 %collective-permute-start.5 = (f32[8,32]{1,0:T(8,128)S(1)}, f32[8,32]{1,0:T(8,128)S(1)}, u32[]{:S(2)}, u32[]{:S(2)}) collective-permute-start(f32[8,32]{1,0:T(8,128)S(1)} %force_bias.1), channel_id=1, source_target_pairs={{0,2},{1,3},{2,0},{3,1},{4,6},{5,7},{6,4},{7,5},{8,10},{9,11},{10,... | collective-permute-start | bytes 3080 | tf_op jit(solution)/shard_map/ppermute | solution.py:44
  30.2 9.6 %collective-permute-start.8 = (f32[8,32]{1,0:T(8,128)S(1)}, f32[8,32]{1,0:T(8,128)S(1)}, u32[]{:S(2)}, u32[]{:S(2)}) collective-permute-start(f32[8,32]{1,0:T(8,128)S(1)} %add_add_fusion.b0), channel_id=1, source_target_pairs={{0,4},{1,5},{2,6},{3,7},{4,8},{5,9},{6,10},{7,11},{8,12},{9,13},{1... | collective-permute-start | bytes 3080 | tf_op jit(solution)/shard_map/ppermute | solution.py:48
  33.1 6.7 %collective-permute-start.9 = (f32[8,32]{1,0:T(8,128)S(1)}, f32[8,32]{1,0:T(8,128)S(1)}, u32[]{:S(2)}, u32[]{:S(2)}) collective-permute-start(f32[8,32]{1,0:T(8,128)S(1)} %add_add_fusion.b0), channel_id=1, source_target_pairs={{0,8},{1,9},{2,10},{3,11},{4,12},{5,13},{6,14},{7,15},{8,0},{9,1},... | collective-permute-start | bytes 3080 | tf_op jit(solution)/shard_map/ppermute | solution.py:48
  37.3 3.4 %collective-permute-start.10 = (f32[8,32]{1,0:T(8,128)S(1)}, f32[8,32]{1,0:T(8,128)S(1)}, u32[]{:S(2)}, u32[]{:S(2)}) collective-permute-start(f32[8,32]{1,0:T(8,128)S(1)} %add_add_fusion.b0), channel_id=1, source_target_pairs={{0,12},{1,13},{2,14},{3,15},{4,0},{5,1},{6,2},{7,3},{8,4},{9,5},{1... | collective-permute-start | bytes 3080 | tf_op jit(solution)/shard_map/ppermute | solution.py:48
  40.7 2.5 %copy-start.1 = (bf16[16,100,1600]{2,0,1:T(8,128)(2,1)S(1)}, bf16[16,100,1600]{2,0,1:T(8,128)(2,1)}, u32[]{:S(2)}) copy-start(bf16[16,100,1600]{2,0,1:T(8,128)(2,1)} %param.7) | copy-start | bytes 15360004
  47.4 25.8 %collective-permute-start.17 = (bf16[4,50,1600]{2,0,1:T(4,128)(2,1)S(1)}, bf16[4,50,1600]{2,0,1:T(4,128)(2,1)S(1)}, u32[]{:S(2)}, u32[]{:S(2)}) collective-permute-start(bf16[4,50,1600]{2,0,1:T(4,128)(2,1)S(1)} %copy.22), channel_id=1, source_target_pairs={{0,32},{16,48},{32,0},{48,16},{64,96},{80,112},{96,64},{112,80},{1... | collective-permute-start | bytes 1920008 | tf_op jit(solution)/shard_map/ppermute | solution.py:36
  54.7 13.5 %collective-permute-start.13 = (bf16[2,50,1600]{2,1,0:T(8,128)(2,1)S(1)}, bf16[2,50,1600]{2,1,0:T(8,128)(2,1)S(1)}, u32[]{:S(2)}, u32[]{:S(2)}) collective-permute-start(bf16[2,50,1600]{2,1,0:T(8,128)(2,1)S(1)} %get-tuple-element.19), channel_id=1, source_target_pairs={{0,64},{16,80},{32,96},{48,112},{64,128},{80,144},{96,160},{112,17... | collective-permute-start | bytes 960008 | tf_op jit(solution)/shard_map/ppermute | solution.py:32
  54.8 13.4 %collective-permute-start.14 = (bf16[2,50,1600]{2,1,0:T(8,128)(2,1)S(1)}, bf16[2,50,1600]{2,1,0:T(8,128)(2,1)S(1)}, u32[]{:S(2)}, u32[]{:S(2)}) collective-permute-start(bf16[2,50,1600]{2,1,0:T(8,128)(2,1)S(1)} %get-tuple-element.20), channel_id=1, source_target_pairs={{0,128},{16,144},{32,160},{48,176},{64,192},{80,208},{96,224},{112... | collective-permute-start | bytes 960008 | tf_op jit(solution)/shard_map/ppermute | solution.py:32
  55.3 17.0 %collective-permute-start.15 = (bf16[2,50,1600]{2,1,0:T(8,128)(2,1)S(1)}, bf16[2,50,1600]{2,1,0:T(8,128)(2,1)S(1)}, u32[]{:S(2)}, u32[]{:S(2)}) collective-permute-start(bf16[2,50,1600]{2,1,0:T(8,128)(2,1)S(1)} %get-tuple-element.21), channel_id=1, source_target_pairs={{0,192},{16,208},{32,224},{48,240},{64,0},{80,16},{96,32},{112,48}... | collective-permute-start | bytes 960008 | tf_op jit(solution)/shard_map/ppermute | solution.py:32
  72.4 6.3 %collective-permute-start.16 = (bf16[50,1600]{1,0:T(8,128)(2,1)S(1)}, bf16[50,1600]{1,0:T(8,128)(2,1)S(1)}, u32[]{:S(2)}, u32[]{:S(2)}) collective-permute-start(bf16[50,1600]{1,0:T(8,128)(2,1)S(1)} %x_sum.1), channel_id=1, source_target_pairs={{0,32},{16,48},{32,0},{48,16},{64,96},{80,112},{96,64},{112,80},{1... | collective-permute-start | bytes 480008 | tf_op jit(solution)/shard_map/ppermute | solution.py:36
  74.1 6.6 %collective-permute-start.18 = (bf16[50,1600]{1,0:T(8,128)(2,1)}, bf16[50,1600]{1,0:T(8,128)(2,1)S(1)}, u32[]{:S(2)}, u32[]{:S(2)}) collective-permute-start(bf16[50,1600]{1,0:T(8,128)(2,1)} %get-tuple-element.25), channel_id=1, source_target_pairs={{0,64},{16,80},{32,96},{48,112},{64,128},{80,144},{96,160},{112,17... | collective-permute-start | bytes 480008 | tf_op jit(solution)/shard_map/ppermute | solution.py:32
  74.7 10.2 %collective-permute-start.19 = (bf16[50,1600]{1,0:T(8,128)(2,1)}, bf16[50,1600]{1,0:T(8,128)(2,1)S(1)}, u32[]{:S(2)}, u32[]{:S(2)}) collective-permute-start(bf16[50,1600]{1,0:T(8,128)(2,1)} %get-tuple-element.26), channel_id=1, source_target_pairs={{0,128},{16,144},{32,160},{48,176},{64,192},{80,208},{96,224},{112... | collective-permute-start | bytes 480008 | tf_op jit(solution)/shard_map/ppermute | solution.py:32
  78.7 6.3 %collective-permute-start.20 = (bf16[50,1600]{1,0:T(8,128)(2,1)S(1)}, bf16[50,1600]{1,0:T(8,128)(2,1)S(1)}, u32[]{:S(2)}, u32[]{:S(2)}) collective-permute-start(bf16[50,1600]{1,0:T(8,128)(2,1)S(1)} %get-tuple-element.27), channel_id=1, source_target_pairs={{0,192},{16,208},{32,224},{48,240},{64,0},{80,16},{96,32},{112,48}... | collective-permute-start | bytes 480008 | tf_op jit(solution)/shard_map/ppermute | solution.py:32
  85.7 15.0 %collective-permute-start.21 = (bf16[50,1600]{1,0:T(8,128)(2,1)S(1)}, bf16[50,1600]{1,0:T(8,128)(2,1)S(1)}, u32[]{:S(2)}, u32[]{:S(2)}) collective-permute-start(bf16[50,1600]{1,0:T(8,128)(2,1)S(1)} %get-tuple-element.29), channel_id=1, source_target_pairs={{0,8},{1,9},{2,10},{3,11},{4,16},{5,17},{6,18},{7,19},{8,0},{9,1},... | collective-permute-start | bytes 480008 | tf_op jit(solution)/shard_map/ppermute | solution.py:61
  93.4 11.0 %collective-permute-start.26 = (bf16[50,1600]{1,0:T(8,128)(2,1)S(1)}, bf16[50,1600]{1,0:T(8,128)(2,1)S(1)}, u32[]{:S(2)}, u32[]{:S(2)}) collective-permute-start(bf16[50,1600]{1,0:T(8,128)(2,1)S(1)} %get-tuple-element.28), channel_id=1, source_target_pairs={{4,24},{5,25},{6,26},{7,27},{12,16},{13,17},{14,18},{15,19},{16,4}... | collective-permute-start | bytes 480008 | tf_op jit(solution)/shard_map/ppermute | solution.py:61
  104.5 10.9 %collective-permute-start.27 = (bf16[50,1600]{1,0:T(8,128)(2,1)S(1)}, bf16[50,1600]{1,0:T(8,128)(2,1)S(1)}, u32[]{:S(2)}, u32[]{:S(2)}) collective-permute-start(bf16[50,1600]{1,0:T(8,128)(2,1)S(1)} %get-tuple-element.39.refs_0_), channel_id=1, source_target_pairs={{0,1},{1,2},{2,3},{3,0},{4,5},{5,6},{6,7},{7,4},{8,9},{9,10},{10,1... | collective-permute-start | bytes 480008 | tf_op jit(solution)/shard_map/ppermute | solution.py:44
  104.6 10.8 %collective-permute-start.28 = (bf16[50,1600]{1,0:T(8,128)(2,1)S(1)}, bf16[50,1600]{1,0:T(8,128)(2,1)S(1)}, u32[]{:S(2)}, u32[]{:S(2)}) collective-permute-start(bf16[50,1600]{1,0:T(8,128)(2,1)S(1)} %get-tuple-element.39.refs_0_), channel_id=1, source_target_pairs={{0,2},{1,3},{2,0},{3,1},{4,6},{5,7},{6,4},{7,5},{8,10},{9,11},{10,... | collective-permute-start | bytes 480008 | tf_op jit(solution)/shard_map/ppermute | solution.py:44
  107.1 9.2 %collective-permute-start.29 = (bf16[50,1600]{1,0:T(8,128)(2,1)S(1)}, bf16[50,1600]{1,0:T(8,128)(2,1)S(1)}, u32[]{:S(2)}, u32[]{:S(2)}) collective-permute-start(bf16[50,1600]{1,0:T(8,128)(2,1)S(1)} %get-tuple-element.39.refs_0_), channel_id=1, source_target_pairs={{0,3},{1,0},{2,1},{3,2},{4,7},{5,4},{6,5},{7,6},{8,11},{9,8},{10,9... | collective-permute-start | bytes 480008 | tf_op jit(solution)/shard_map/ppermute | solution.py:44
  117.5 27.0 %collective-permute-start.30 = (bf16[4,50,1600]{2,0,1:T(4,128)(2,1)}, bf16[4,50,1600]{2,0,1:T(4,128)(2,1)}, u32[]{:S(2)}, u32[]{:S(2)}) collective-permute-start(bf16[4,50,1600]{2,0,1:T(4,128)(2,1)} %copy.24), channel_id=1, source_target_pairs={{0,32},{16,48},{32,0},{48,16},{64,96},{80,112},{96,64},{112,80},{1... | collective-permute-start | bytes 1920008 | tf_op jit(solution)/shard_map/ppermute | solution.py:36
  117.7 16.0 %collective-permute-start.37 = (bf16[100,200]{1,0:T(8,128)(2,1)S(1)}, bf16[100,200]{1,0:T(8,128)(2,1)S(1)}, u32[]{:S(2)}, u32[]{:S(2)}) collective-permute-start(bf16[100,200]{1,0:T(8,128)(2,1)S(1)} %bitcast.34), channel_id=1, source_target_pairs={{0,0},{1,1},{2,2},{3,3},{4,16},{5,17},{6,18},{7,19},{8,32},{9,33},... | collective-permute-start | bytes 120008 | tf_op jit(solution)/shard_map/ppermute | solution.py:61
  133.7 1.2 collective-permute-start.38
  135.0 4.5 %collective-permute-start.39 = (bf16[2,100,200]{2,1,0:T(8,128)(2,1)S(1)}, bf16[2,100,200]{2,1,0:T(8,128)(2,1)S(1)}, u32[]{:S(2)}, u32[]{:S(2)}) collective-permute-start(bf16[2,100,200]{2,1,0:T(8,128)(2,1)S(1)} %pad_maximum_fusion.1), channel_id=1, source_target_pairs={{0,32},{16,48},{32,0},{48,16},{64,96},{80,112},{96,64},{112,80},{1... | collective-permute-start | bytes 240008 | tf_op jit(solution)/shard_map/ppermute | solution.py:36
  136.3 36.4 %collective-permute-start.35 = (bf16[4,50,1600]{2,0,1:T(4,128)(2,1)}, bf16[4,50,1600]{2,0,1:T(4,128)(2,1)}, u32[]{:S(2)}, u32[]{:S(2)}) collective-permute-start(bf16[4,50,1600]{2,0,1:T(4,128)(2,1)} %copy.24), channel_id=1, source_target_pairs={{0,16},{16,0},{32,48},{48,32},{64,80},{80,64},{96,112},{112,96},{1... | collective-permute-start | bytes 1920008 | tf_op jit(solution)/shard_map/ppermute | solution.py:40
  139.6 11.5 %collective-permute-start.40 = (bf16[4,100,200]{2,1,0:T(8,128)(2,1)S(1)}, bf16[4,100,200]{2,1,0:T(8,128)(2,1)S(1)}, u32[]{:S(2)}, u32[]{:S(2)}) collective-permute-start(bf16[4,100,200]{2,1,0:T(8,128)(2,1)S(1)} %pad_maximum_fusion.refs_12_), channel_id=1, source_target_pairs={{0,1},{1,2},{2,3},{3,0},{4,5},{5,6},{6,7},{7,4},{8,9},{9,10},{10,1... | collective-permute-start | bytes 480008 | tf_op jit(solution)/shard_map/ppermute | solution.py:44
  140.7 12.6 %collective-permute-start.41 = (bf16[4,100,200]{2,1,0:T(8,128)(2,1)S(1)}, bf16[4,100,200]{2,1,0:T(8,128)(2,1)S(1)}, u32[]{:S(2)}, u32[]{:S(2)}) collective-permute-start(bf16[4,100,200]{2,1,0:T(8,128)(2,1)S(1)} %pad_maximum_fusion.refs_12_), channel_id=1, source_target_pairs={{0,2},{1,3},{2,0},{3,1},{4,6},{5,7},{6,4},{7,5},{8,10},{9,11},{10,... | collective-permute-start | bytes 480008 | tf_op jit(solution)/shard_map/ppermute | solution.py:44
  143.1 4.7 %collective-permute-start.22 = (bf16[50,1600]{1,0:T(8,128)(2,1)S(1)}, bf16[50,1600]{1,0:T(8,128)(2,1)S(1)}, u32[]{:S(2)}, u32[]{:S(2)}) collective-permute-start(bf16[50,1600]{1,0:T(8,128)(2,1)S(1)} %get-tuple-element.40.refs_0_), channel_id=1, source_target_pairs={{0,32},{16,48},{32,0},{48,16},{64,96},{80,112},{96,64},{112,80},{1... | collective-permute-start | bytes 480008 | tf_op jit(solution)/shard_map/ppermute | solution.py:36
  144.5 28.2 %collective-permute-start.36 = (bf16[4,50,1600]{2,0,1:T(4,128)(2,1)}, bf16[4,50,1600]{2,0,1:T(4,128)(2,1)}, u32[]{:S(2)}, u32[]{:S(2)}) collective-permute-start(bf16[4,50,1600]{2,0,1:T(4,128)(2,1)} %collective-permute-done.30), channel_id=1, source_target_pairs={{0,16},{16,0},{32,48},{48,32},{64,80},{80,64},{96,112},{112,96},{1... | collective-permute-start | bytes 1920008 | tf_op jit(solution)/shard_map/ppermute | solution.py:40
  147.8 3.2 %collective-permute-start.44 = (f32[8,16]{1,0:T(8,128)S(1)}, f32[8,16]{1,0:T(8,128)S(1)}, u32[]{:S(2)}, u32[]{:S(2)}) collective-permute-start(f32[8,16]{1,0:T(8,128)S(1)} %get-tuple-element.44), channel_id=1, source_target_pairs={{0,16},{16,0},{32,48},{48,32},{64,80},{80,64},{96,112},{112,96},{1... | collective-permute-start | bytes 1544 | tf_op jit(solution)/shard_map/ppermute | solution.py:40
  151.1 19.1 %collective-permute-start.23 = (bf16[2,50,1600]{2,1,0:T(8,128)(2,1)S(1)}, bf16[2,50,1600]{2,1,0:T(8,128)(2,1)S(1)}, u32[]{:S(2)}, u32[]{:S(2)}) collective-permute-start(bf16[2,50,1600]{2,1,0:T(8,128)(2,1)S(1)} %stack_low.1.refs_0_), channel_id=1, source_target_pairs={{0,1},{1,2},{2,3},{3,0},{4,5},{5,6},{6,7},{7,4},{8,9},{9,10},{10,1... | collective-permute-start | bytes 960008 | tf_op jit(solution)/shard_map/ppermute | solution.py:44
  151.1 0.7 copy-start.2
  151.8 19.6 %collective-permute-start.24 = (bf16[2,50,1600]{2,1,0:T(8,128)(2,1)S(1)}, bf16[2,50,1600]{2,1,0:T(8,128)(2,1)S(1)}, u32[]{:S(2)}, u32[]{:S(2)}) collective-permute-start(bf16[2,50,1600]{2,1,0:T(8,128)(2,1)S(1)} %stack_low.1.refs_0_), channel_id=1, source_target_pairs={{0,2},{1,3},{2,0},{3,1},{4,6},{5,7},{6,4},{7,5},{8,10},{9,11},{10,... | collective-permute-start | bytes 960008 | tf_op jit(solution)/shard_map/ppermute | solution.py:44
  153.2 0.7 copy-start.4
  153.9 17.4 %collective-permute-start.25 = (bf16[2,50,1600]{2,1,0:T(8,128)(2,1)S(1)}, bf16[2,50,1600]{2,1,0:T(8,128)(2,1)S(1)}, u32[]{:S(2)}, u32[]{:S(2)}) collective-permute-start(bf16[2,50,1600]{2,1,0:T(8,128)(2,1)S(1)} %stack_low.1.refs_0_), channel_id=1, source_target_pairs={{0,3},{1,0},{2,1},{3,2},{4,7},{5,4},{6,5},{7,6},{8,11},{9,8},{10,9... | collective-permute-start | bytes 960008 | tf_op jit(solution)/shard_map/ppermute | solution.py:44
  170.2 10.3 %collective-permute-start.31 = (bf16[2,50,1600]{2,1,0:T(8,128)(2,1)S(1)}, bf16[2,50,1600]{2,1,0:T(8,128)(2,1)S(1)}, u32[]{:S(2)}, u32[]{:S(2)}) collective-permute-start(bf16[2,50,1600]{2,1,0:T(8,128)(2,1)S(1)} %stack_low.1.refs_0_), channel_id=1, source_target_pairs={{0,16},{16,0},{32,48},{48,32},{64,80},{80,64},{96,112},{112,96},{1... | collective-permute-start | bytes 960008 | tf_op jit(solution)/shard_map/ppermute | solution.py:40
  171.4 9.1 %collective-permute-start.32 = (bf16[2,50,1600]{2,1,0:T(8,128)(2,1)S(1)}, bf16[2,50,1600]{2,1,0:T(8,128)(2,1)}, u32[]{:S(2)}, u32[]{:S(2)}) collective-permute-start(bf16[2,50,1600]{2,1,0:T(8,128)(2,1)S(1)} %collective-permute-done.23.refs_1_), channel_id=1, source_target_pairs={{0,16},{16,0},{32,48},{48,32},{64,80},{80,64},{96,112},{112,96},{1... | collective-permute-start | bytes 960008 | tf_op jit(solution)/shard_map/ppermute | solution.py:40
  171.4 9.1 %collective-permute-start.33 = (bf16[2,50,1600]{2,1,0:T(8,128)(2,1)S(1)}, bf16[2,50,1600]{2,1,0:T(8,128)(2,1)}, u32[]{:S(2)}, u32[]{:S(2)}) collective-permute-start(bf16[2,50,1600]{2,1,0:T(8,128)(2,1)S(1)} %collective-permute-done.24.refs_2_), channel_id=1, source_target_pairs={{0,16},{16,0},{32,48},{48,32},{64,80},{80,64},{96,112},{112,96},{1... | collective-permute-start | bytes 960008 | tf_op jit(solution)/shard_map/ppermute | solution.py:40
  172.7 7.8 %collective-permute-start.34 = (bf16[2,50,1600]{2,1,0:T(8,128)(2,1)S(1)}, bf16[2,50,1600]{2,1,0:T(8,128)(2,1)}, u32[]{:S(2)}, u32[]{:S(2)}) collective-permute-start(bf16[2,50,1600]{2,1,0:T(8,128)(2,1)S(1)} %collective-permute-done.25.refs_3_), channel_id=1, source_target_pairs={{0,16},{16,0},{32,48},{48,32},{64,80},{80,64},{96,112},{112,96},{1... | collective-permute-start | bytes 960008 | tf_op jit(solution)/shard_map/ppermute | solution.py:40
  172.7 7.8 %collective-permute-start.42 = (bf16[4,100,200]{2,1,0:T(8,128)(2,1)S(1)}, bf16[4,100,200]{2,1,0:T(8,128)(2,1)}, u32[]{:S(2)}, u32[]{:S(2)}) collective-permute-start(bf16[4,100,200]{2,1,0:T(8,128)(2,1)S(1)} %pad_maximum_fusion.refs_12_), channel_id=1, source_target_pairs={{0,3},{1,0},{2,1},{3,2},{4,7},{5,4},{6,5},{7,6},{8,11},{9,8},{10,9... | collective-permute-start | bytes 480008 | tf_op jit(solution)/shard_map/ppermute | solution.py:44
  180.5 0.9 copy-start.3
  181.4 0.9 copy-start.5
  199.8 9.6 %collective-permute-start.43 = (bf16[100,200]{1,0:T(8,128)(2,1)S(1)}, bf16[100,200]{1,0:T(8,128)(2,1)S(1)}, u32[]{:S(2)}, u32[]{:S(2)}) collective-permute-start(bf16[100,200]{1,0:T(8,128)(2,1)S(1)} %taylor.1), channel_id=1, source_target_pairs={{0,0},{1,1},{2,2},{3,3},{4,16},{5,17},{6,18},{7,19},{8,32},{9,33},... | collective-permute-start | bytes 120008 | tf_op jit(solution)/shard_map/ppermute | solution.py:61
where the time goes:
time: 211 us; the launch traced here: 210 us
  waiting for transfers between devices  85.8 us (41%)
  starting transfers between devices  71.9 us (34%)
  Pallas kernels  31.1 us (15%)
  local copies, waits for them, and re-layouts  14.6 us (7%)
  matrix products  4.56 us (2%)
    pallas_call x9, Pallas kernels, call(): pl.pallas_call(kernel, out_shape=outs, in_specs=[SMEM] * smem + [VMEM] *...  31.1 us
    ppermute x9, waiting for transfers between devices, send_x(): lax.ppermute(array, 'vec', [(vec_of(*p), vec_of(p[0] + step, p[1], p[2]))...  27.2 us
    ppermute x12, waiting for transfers between devices, send_y(): lax.ppermute(array, 'pair', [(h * NY + y, h * NY + (y + step) % NY) for h...  25.5 us
    ppermute x4, waiting for transfers between devices, everywhere(): return lax.ppermute(array, ('vec', 'pair'), pairs)  24 us
    ppermute x4, starting transfers between devices, everywhere(): return lax.ppermute(array, ('vec', 'pair'), pairs)  19.6 us
    ppermute x12, starting transfers between devices, send_y(): lax.ppermute(array, 'pair', [(h * NY + y, h * NY + (y + step) % NY) for h...  17 us
    ppermute x9, starting transfers between devices, send_x(): lax.ppermute(array, 'vec', [(vec_of(*p), vec_of(p[0] + step, p[1], p[2]))...  10.8 us
    ppermute x3, starting transfers between devices, send_h(): lax.ppermute(array, 'pair', [(h * NY + y, (h + step) % NH * NY + y) for h...  9.55 us
  transfers between devices with their start and end apart: 45, of which 20 were waited for; matrix products, arithmetic and copies ran while one was open for 6% of the time, Pallas kernels for 4%

commit v1 on v0

--- a/solution.py
+++ b/solution.py
@@ -16,6 +16,7 @@
 shift_cap = 1.0
 
 VMEM = pl.BlockSpec(memory_space=pltpu.VMEM)
+FAR = pl.BlockSpec(memory_space=pl.ANY)
 SMEM = pl.BlockSpec(memory_space=pltpu.SMEM)
 NT = (((1,), (1,)), ((), ()))
 
@@ -85,7 +86,17 @@
     return [(start, min(GROUP, rows - start)) for start in range(0, rows, GROUP)]
 
 
-def bias_kernel(r0, r1, r2, r3, own, other, out_ref):
+def factor_kernel(after, trial, block, out_ref):
+    count, vectors, depth = block.shape
+    product = jnp.dot(
+        block[...].reshape(count * vectors, depth), trial[...], preferred_element_type=jnp.float32
+    ).astype(jnp.bfloat16)
+    out_ref[...] = product.reshape(count, vectors, trial.shape[1])
+
+
+def bias_kernel(r0, r1, r2, r3, own, other, walker, neighbour, out_ref, stacked):
+    stacked[: walker.shape[0], :] = walker[...]
+    stacked[walker.shape[0] :, :] = neighbour[...]
     rows, vectors, depth = own.shape
     parts = []
     for factor in (own, other):
@@ -142,62 +153,76 @@
     return blocks
 
 
-def walker_sums(blocks, own, other, base, half, walkers, store):
-    vectors, columns = own.shape[1:]
-    for start, count in groups_of(half):
+def walker_sums(blocks, held, copies, other, base, store):
+    half, vectors, columns = held.shape
+    for (start, count), copy in zip(groups_of(half), copies):
+        copy.wait()
         depth = count * vectors
-        lefts = [
-            jnp.concatenate([block[w * GROUP : (w + 1) * GROUP, :depth] for w in walkers], axis=0) for block in blocks
-        ]
         for left in range(0, columns, 512):
             right = min(columns, left + 512)
-            total = 0.0
-            for block, source in zip(lefts, (own, other)):
-                total = total + jnp.dot(
-                    block,
-                    source[pl.ds(base + start, count), :, left:right].reshape(depth, right - left),
-                    preferred_element_type=jnp.float32,
-                )
+            total = jnp.dot(
+                blocks[0][:, :depth],
+                held[start : start + count, :, left:right].reshape(depth, right - left),
+                preferred_element_type=jnp.float32,
+            ) + jnp.dot(
+                blocks[1][:, :depth],
+                other[pl.ds(base + start, count), :, left:right].reshape(depth, right - left),
+                preferred_element_type=jnp.float32,
+            )
             total = total.astype(jnp.bfloat16)
-            for at, walker in enumerate(walkers):
-                store(walker, start, count, left, right, total[at * GROUP : at * GROUP + count, :])
-
-
-ODD = [step * NL + 1 for step in range(NX)]
-EVEN = [step * NL for step in range(NX)]
-
-
-def send_kernel(at, b0, b1, b2, b3, aux, own, other, fields_ref, send_ref):
-    half = own.shape[0] // NL
+            for walker in ALL:
+                store(walker, start, count, left, right, total[walker * GROUP : walker * GROUP + count, :])
+
+
+ALL = list(range(NX * NL))
+
+
+def fetch(source, base, held, sems):
+    copies = []
+    for at, (start, count) in enumerate(groups_of(held.shape[0])):
+        copy = pltpu.make_async_copy(
+            source.at[pl.ds(base + start, count)], held.at[pl.ds(start, count)], sems.at[at]
+        )
+        copy.start()
+        copies.append(copy)
+    return copies
+
+
+def away_kernel(at, b0, b1, b2, b3, aux, own, other, after, fields_ref, even_ref, odd_ref, held, sems):
+    half = held.shape[0]
+    base = (1 - at[0]) * half
+    copies = fetch(own, base, held, sems)
     fields = coefficients_of((b0, b1, b2, b3), aux)
     fields_ref[...] = fields
     blocks = block_diagonals((root_step * fields).astype(jnp.bfloat16), own.shape[1])
 
     def store(walker, start, count, left, right, value):
-        send_ref[walker // NL, start : start + count, left:right] = value
-
-    walker_sums(blocks, own, other, (1 - at[0]) * half, half, ODD, store)
-
-
-def keep_kernel(at, fields, own, other, p0, p1, p2, p3, keep_ref):
-    half = own.shape[0] // NL
+        out = odd_ref if walker % NL else even_ref
+        row = walker // NL * half + start
+        out[row : row + count, left:right] = value
+
+    walker_sums(blocks, held, copies, other, base, store)
+
+
+def keep_kernel(at, fields, even, walkers, partner, own, other, p0, p1, p2, p3, odd_ref, stacked, held, sems):
+    half = held.shape[0]
+    base = at[0] * half
+    copies = fetch(own, base, held, sems)
     blocks = block_diagonals((root_step * fields[...]).astype(jnp.bfloat16), own.shape[1])
     outs = (p0, p1, p2, p3)
-
-    def store_even(side):
-        def store(walker, start, count, left, right, value):
-            outs[walker // NL][side, start : start + count, left:right] = value
-
-        return store
-
-    def store_all(walker, start, count, left, right, value):
-        if walker % NL == 0:
-            outs[walker // NL][0, start : start + count, left:right] = value
+    for step, out in enumerate(outs):
+        out[half:, :] = even[step * half : (step + 1) * half, :]
+    stacked[: walkers.shape[0], :] = walkers[...]
+    stacked[walkers.shape[0] :, :] = partner[...]
+
+    def store(walker, start, count, left, right, value):
+        if walker % NL:
+            row = walker // NL * half + start
+            odd_ref[row : row + count, left:right] = value
         else:
-            keep_ref[walker // NL, start : start + count, left:right] = value
-
-    walker_sums(blocks, own, other, (1 - at[0]) * half, half, EVEN, store_even(1))
-    walker_sums(blocks, own, other, at[0] * half, half, EVEN + ODD, store_all)
+            outs[walker // NL][start : start + count, left:right] = value
+
+    walker_sums(blocks, held, copies, other, base, store)
 
 
 def wide(value):
@@ -205,16 +230,24 @@
 
 
 def pair_sum_kernel(keep, arrived, o0, o1, o2, o3):
+    half = o0.shape[0]
     for step, out in enumerate((o0, o1, o2, o3)):
-        out[...] = (wide(keep[step]) + wide(arrived[step])).astype(out.dtype)
+        rows = slice(step * half, (step + 1) * half)
+        out[...] = (wide(keep[rows, :]) + wide(arrived[rows, :])).astype(out.dtype)
 
 
 def x_sum_kernel(p0, p1, p2, p3, out):
-    out[...] = ((wide(p0[1]) + wide(p1[1])) + (wide(p2[1]) + wide(p3[1]))).astype(out.dtype)
-
-
-def last_sum_kernel(at, p0, p1, p2, p3, arrived, q0, q1, q2, q3, first, second):
-    even = ((wide(p0[0]) + wide(p1[0])) + (wide(p2[0]) + wide(p3[0]))) + wide(arrived[...])
+    half = out.shape[0]
+    out[...] = (
+        (wide(p0[half:, :]) + wide(p1[half:, :])) + (wide(p2[half:, :]) + wide(p3[half:, :]))
+    ).astype(out.dtype)
+
+
+def last_sum_kernel(at, p0, p1, p2, p3, arrived, q0, q1, q2, q3, w1, w2, w3, first, second):
+    half = first.shape[0]
+    even = (
+        (wide(p0[:half, :]) + wide(p1[:half, :])) + (wide(p2[:half, :]) + wide(p3[:half, :]))
+    ) + wide(arrived[...])
     odd = (wide(q0[...]) + wide(q1[...])) + (wide(q2[...]) + wide(q3[...]))
     turn = (at[0] - at[1] + NH) % NH
     pick = jnp.logical_or(turn == 1, turn == 2)
@@ -222,9 +255,25 @@
     second[...] = jnp.where(pick, odd, even).astype(second.dtype)
 
 
-def stack_kernel(*refs):
-    for step, ref in enumerate(refs[:-1]):
-        refs[-1][step] = ref[...]
+def choose_kernel(at, second, got, more, block0, block1):
+    active = (at[0] + at[1]) % 2 == 0
+
+    @pl.when(active)
+    def _():
+        block0[...] = second[...]
+        block1[...] = got[...]
+
+    @pl.when(jnp.logical_not(active))
+    def _():
+        block0[...] = got[...]
+        block1[...] = more[...]
+
+
+def stack_kernel(*refs, after=0):
+    sources, out = refs[: len(refs) - 1 - after], refs[-1]
+    half = sources[0].shape[0]
+    for step, ref in enumerate(sources):
+        out[step * half : (step + 1) * half, :] = ref[...]
 
 
 def taylor_kernel(at, *refs):
@@ -237,32 +286,29 @@
         mine = pieces[side * 6 : side * 6 + 6]
         for step in range(NY):
             row = ((base % NH) * NY + (y - step + NY) % NY) * NL
-            held[row + low] = mine[step][0]
-            held[row + 1 - low] = mine[step][1]
+            held[row + low] = mine[step][:half, :]
+            held[row + 1 - low] = mine[step][half:, :]
             row = (((base + 2) % NH) * NY + (y - step + NY) % NY) * NL
-            held[row + low] = mine[4][step]
-            held[row + 1 - low] = mine[5][step]
+            held[row + low] = mine[4][step * half : (step + 1) * half, :]
+            held[row + 1 - low] = mine[5][step * half : (step + 1) * half, :]
     for block in range(NH * NY * NL):
         operator[block * half : (block + 1) * half, :] = held[block]
     spread = terms.shape[2]
     for step, ref in enumerate((w0, w1, w2, w3)):
-        total[step] = ref[...]
+        for at_row in range(NL * NC):
+            total[step, at_row] = ref[at_row * rows : (at_row + 1) * rows, :]
     for block in range(NH * NY):
         piece = total[
             (y - block % NY + NY) % NY, (((block // NY // NC) ^ low) * NC + ((block // NY % NC) ^ core))
         ]
         terms[0, block * rows : (block + 1) * rows, :] = piece
-    chunk = 400
     mine = low * NC + core
 
     def one_term(degree, accumulated):
         source = (degree - 1) % 2
 
-        @pl.loop(0, operator.shape[0] // chunk)
-        def _(index):
-            place = pl.ds(pl.multiple_of(index * chunk, 16), chunk)
-            product = jnp.dot(operator[place, :], terms[source], preferred_element_type=jnp.float32)
-            terms[1 - source, place, :] = (product / degree.astype(jnp.float32)).astype(jnp.bfloat16)
+        product = jnp.dot(operator[...], terms[source], preferred_element_type=jnp.float32)
+        terms[1 - source] = (product / degree.astype(jnp.float32)).astype(jnp.bfloat16)
 
         picked = jnp.zeros((rows, spread), jnp.float32)
         for block in range(NH * NY):
@@ -270,18 +316,21 @@
             picked = jnp.where(mine * NY + y == block, piece, picked)
         return accumulated + picked
 
-    accumulated = lax.fori_loop(1, TAYLOR + 1, one_term, wide(w0[0]))
+    accumulated = lax.fori_loop(1, TAYLOR + 1, one_term, wide(w0[:rows, :]))
     out_ref[...] = accumulated.astype(out_ref.dtype)
 
 
-def call(kernel, outs, args, name, scratch=(), smem=0):
+def call(kernel, outs, args, name, scratch=(), smem=0, idle=0, far=(), limit=16):
+    specs = [SMEM] * smem + [VMEM] * (len(args) - smem - idle) + [FAR] * idle
+    for at in far:
+        specs[at] = FAR
     return pl.pallas_call(
         kernel,
         out_shape=outs,
-        in_specs=[SMEM] * smem + [VMEM] * (len(args) - smem),
+        in_specs=specs,
         out_specs=[VMEM] * len(outs) if isinstance(outs, (list, tuple)) else VMEM,
         scratch_shapes=list(scratch),
-        compiler_params=pltpu.CompilerParams(vmem_limit_bytes=48 * 2**20),
+        compiler_params=pltpu.CompilerParams(vmem_limit_bytes=limit * 2**20),
         name=name,
     )(*args)
 
@@ -290,7 +339,8 @@
     vectors, rows, orbitals = cholesky.shape
     occupied = walkers.shape[2]
     half = rows // NL
-    bf16 = jnp.bfloat16
+    bf16, f32 = jnp.bfloat16, jnp.float32
+    shaped = jax.ShapeDtypeStruct
     me = lax.axis_index("vec")
     x, low, core = me // (NL * NC), (me // NC) % NL, me % NC
     pair = lax.axis_index("pair")
@@ -299,23 +349,41 @@
     own = jnp.transpose(cholesky, (1, 0, 2))
     other = swap_core(own)
     aux_other = swap_core(aux_fields)
+    rows_here = exchange(walkers[0])
 
     rotated = jnp.dot(
-        walkers[0].astype(jnp.float32), inv_correlation[0], precision=lax.Precision.HIGHEST
+        walkers[0].astype(f32), inv_correlation[0], precision=lax.Precision.HIGHEST
     ).astype(bf16)
     rotated = jnp.pad(rotated, ((0, -rows % GROUP), (0, 0)))
     partner = swap_low(rotated)
+    count = 20
+    factor = pl.pallas_call(
+        factor_kernel,
+        out_shape=shaped((rows, vectors, occupied), bf16),
+        grid=(rows // count,),
+        in_specs=[
+            FAR,
+            pl.BlockSpec((orbitals, occupied), lambda i: (0, 0)),
+            pl.BlockSpec((count, vectors, orbitals), lambda i: (i, 0, 0)),
+        ],
+        out_specs=pl.BlockSpec((count, vectors, occupied), lambda i: (i, 0, 0)),
+        compiler_params=pltpu.CompilerParams(vmem_limit_bytes=16 * 2**20),
+        cost_estimate=pl.CostEstimate(
+            flops=2 * rows * vectors * orbitals * occupied, bytes_accessed=8 * 10**6, transcendentals=0
+        ),
+        name="vector_factor",
+    )(rotated, trial_orbitals, own)
     both = jnp.where(low == 0, jnp.stack([rotated, partner]), jnp.stack([partner, rotated]))
     met = [both] + [send_x(both, -step) for step in range(1, NX)]
 
-    factor = jnp.einsum("pgq,qm->pgm", own, trial_orbitals, preferred_element_type=jnp.float32).astype(bf16)
-    bias = call(
+    bias, two_rows = call(
         bias_kernel,
-        jax.ShapeDtypeStruct((8, 2 * vectors), jnp.float32),
-        (*met, factor, swap_core(factor)),
+        [shaped((8, 2 * vectors), f32), shaped((2 * rows, occupied), bf16)],
+        (*met, factor, swap_core(factor), rows_here, swap_core(rows_here)),
         "force_bias",
     )
     from_y = [bias] + [send_y(bias, step) for step in range(1, NY)]
+    rows_low = swap_low(two_rows)
     bias = (from_y[0] + from_y[2]) + (from_y[1] + from_y[3])
     from_h = [bias] + [send_h(bias, step) for step in range(1, NH)]
 
@@ -323,25 +391,38 @@
     mine = vec_of(x + order // NL, order % NL, core)
     aux = jnp.concatenate([jnp.take(aux_fields, mine, axis=0), jnp.take(aux_other, mine, axis=0)], axis=1)
 
-    piece = jax.ShapeDtypeStruct((half, orbitals), bf16)
-    quad = jax.ShapeDtypeStruct((NX, half, orbitals), bf16)
-    two = jax.ShapeDtypeStruct((2, half, orbitals), bf16)
+    piece, two, quad = [shaped((n * half, orbitals), bf16) for n in (1, 2, 4)]
     where = low.reshape(1).astype(jnp.int32)
-    shifted, away = call(
-        send_kernel,
-        [jax.ShapeDtypeStruct((8, 2 * vectors), jnp.float32), quad],
-        (where, *from_h, aux, own, other),
+    scratch = [pltpu.VMEM((half, vectors, orbitals), bf16), pltpu.SemaphoreType.DMA((len(groups_of(half)),))]
+    shifted, even, away = call(
+        away_kernel,
+        [shaped((8, 2 * vectors), f32), quad, quad],
+        (where, *from_h, aux, own, other, rows_low),
         "operator_away",
+        scratch=scratch,
         smem=1,
+        idle=1,
+        far=(6,),
     )
     away = swap_low(away)
-    *parts, keep = call(keep_kernel, [two] * NX + [quad], (where, shifted, own, other), "operator_keep", smem=1)
+    *parts, keep, four_rows = call(
+        keep_kernel,
+        [two] * NX + [quad, shaped((4 * rows, occupied), bf16)],
+        (where, shifted, even, two_rows, rows_low, own, other),
+        "operator_keep",
+        scratch=scratch,
+        smem=1,
+        far=(5,),
+    )
     parts = [parts[0]] + [send_x(parts[step], step) for step in range(1, NX)]
+    all_rows = [four_rows] + [send_y(four_rows, step) for step in range(1, NY)]
     odd = call(pair_sum_kernel, [piece] * NX, (keep, away), "pair_sum")
     odd = [odd[0]] + [send_x(odd[step], step) for step in range(1, NX)]
     even = swap_low(call(x_sum_kernel, piece, tuple(parts), "x_sum"))
     turn = jnp.stack([high, core]).astype(jnp.int32)
-    first, second = call(last_sum_kernel, [piece] * 2, (turn, *parts, even, *odd), "last_sum", smem=1)
+    first, second = call(
+        last_sum_kernel, [piece] * 2, (turn, *parts, even, *odd, *all_rows[1:]), "last_sum", smem=1, idle=3
+    )
 
     both = jnp.concatenate([shifted[:, :vectors], swap_core(shifted[:, vectors:])])
     walker = jnp.arange(NX * NL * NC)
@@ -350,26 +431,18 @@
     )
     fields = jnp.take(both, place, axis=0)
 
-    late, _ = lax.optimization_barrier((walkers[0], shifted))
-    rows_here = exchange(late)
-    two_rows = jnp.stack([rows_here, swap_core(rows_here)])
-    four_rows = jnp.concatenate([two_rows, swap_low(two_rows)])
-    all_rows = [four_rows] + [send_y(four_rows, step) for step in range(1, NY)]
-
-    active = (high + core) % 2 == 0
     got = everywhere(first, first_target)
     more = everywhere(second, second_target)
-    block0 = jnp.where(active, second, got)
-    block1 = jnp.where(active, got, more)
-    low0 = swap_low(block0)
-    quad1 = call(stack_kernel, quad, (block1, *[send_y(block1, step) for step in range(1, NY)]), "stack_y")
-    pair0 = call(stack_kernel, two, (block0, low0), "stack_low")
+    block0, block1 = call(choose_kernel, [piece] * 2, (turn, second, got, more), "choose", smem=1)
+    pair0 = call(stack_kernel, two, (block0, swap_low(block0)), "stack_low")
+    block1s = [block1] + [send_y(block1, step) for step in range(1, NY)]
+    quad1 = call(functools.partial(stack_kernel, after=1), quad, (*block1s, pair0), "stack_y", idle=1)
     pieces = [pair0] + [send_y(pair0, step) for step in range(1, NY)] + [quad1, swap_low(quad1)]
     pieces = pieces + [swap_core(p) for p in pieces]
     position = jnp.stack([high, y, low, core]).astype(jnp.int32)
     updated = call(
         taylor_kernel,
-        jax.ShapeDtypeStruct((rows, occupied), bf16),
+        shaped((rows, occupied), bf16),
         (position, *pieces, *all_rows),
         "taylor",
         scratch=[
@@ -379,6 +452,7 @@
             pltpu.VMEM((NY, 4, rows, occupied), bf16),
         ],
         smem=1,
+        limit=28,
     )
     return (exchange(updated)[None], fields)
 

time: 211 us -> 177 us (0.84)
  waiting for transfers between devices: 85.8 us -> 62.3 us
  local copies, waits for them, and re-layouts: 14.6 us -> 10.2 us
  matrix products: 4.56 us -> 1.17 us
    ppermute x12, waiting for transfers between devices: 25.5 us -> 14.6 us  [send_y(): lax.ppermute(array, 'pair', [(h * NY + y, h * NY + (y + step) % NY) for h...]
    ppermute x4, waiting for transfers between devices: 24 us -> 16.2 us  [everywhere(): return lax.ppermute(array, ('vec', 'pair'), pairs)]
    ppermute x4 -> x0, local copies, waits for them, and re-layouts: 4.47 us -> none  [the longest x2 3.23 us: swap_core(): lax.ppermute(array, 'vec', [(vec_of(*p), vec_of(p[0], p[1], 1 - p[2])) fo...]
    dot_general x2 -> x1, matrix products: 4.56 us -> 1.17 us  [on_device(): jnp.dot(walkers[0].astype(f32), inv_correlation[0], precision=lax.Precisi...]
    ppermute x6, waiting for transfers between devices: 6.09 us -> 3.27 us  [swap_low(): lax.ppermute(array, 'vec', [(vec_of(*p), vec_of(p[0], 1 - p[1], p[2])) fo...]
    ppermute x4, starting transfers between devices: 19.6 us -> 17.5 us  [everywhere(): return lax.ppermute(array, ('vec', 'pair'), pairs)]
    unnamed x20 -> x17, local copies, waits for them, and re-layouts: 6.88 us -> 8.33 us
    pallas_call x9 -> x11, Pallas kernels: 31.1 us -> 30.2 us  [the longest x10 27.8 us: call(): pl.pallas_call(kernel, out_shape=outs, in_specs=specs, out_specs=[VMEM] *...]
  transfers between devices with their start and end apart: 45 -> 45, of which waited for: 20 -> 23; matrix products, arithmetic and copies ran while one was open for 6% -> 3% of each run, Pallas kernels for 4% -> 6%
where the time goes in v1:
time: 177 us; the launch traced here: 176 us
  starting transfers between devices  70.3 us (40%)
  waiting for transfers between devices  62.3 us (35%)
  Pallas kernels  30.2 us (17%)
  local copies, waits for them, and re-layouts  10.2 us (6%)
    pallas_call x10, Pallas kernels, call(): pl.pallas_call(kernel, out_shape=outs, in_specs=specs, out_specs=[VMEM] *...  27.8 us
    ppermute x9, waiting for transfers between devices, send_x(): lax.ppermute(array, 'vec', [(vec_of(*p), vec_of(p[0] + step, p[1], p[2]))...  26.2 us
    ppermute x4, starting transfers between devices, everywhere(): return lax.ppermute(array, ('vec', 'pair'), pairs)  17.5 us
    ppermute x12, starting transfers between devices, send_y(): lax.ppermute(array, 'pair', [(h * NY + y, h * NY + (y + step) % NY) for h...  16.4 us
    ppermute x4, waiting for transfers between devices, everywhere(): return lax.ppermute(array, ('vec', 'pair'), pairs)  16.2 us
    ppermute x12, waiting for transfers between devices, send_y(): lax.ppermute(array, 'pair', [(h * NY + y, h * NY + (y + step) % NY) for h...  14.6 us
    ppermute x9, starting transfers between devices, send_x(): lax.ppermute(array, 'vec', [(vec_of(*p), vec_of(p[0] + step, p[1], p[2]))...  11 us
    ppermute x11, starting transfers between devices, swap_core(): lax.ppermute(array, 'vec', [(vec_of(*p), vec_of(p[0], p[1], 1 - p[2])) fo...  9.64 us
  transfers between devices with their start and end apart: 45, of which 23 were waited for; matrix products, arithmetic and copies ran while one was open for 3% of the time, Pallas kernels for 6%

profile of v1, /device:TPU:33, one launch (start us, length us, event | category | flops | bytes accessed | tf_op | source)
XLA Modules:
  0.0 176.1 jit_solution(4865254463803893401)
XLA Ops:
  0.7 0.8 collective-permute-start.14
  1.6 1.2 convolution_convert_fusion
  2.9 1.4 copy.13.trial
  4.3 2.5 %copy-done.1 = bf16[16,100,1600]{2,0,1:T(8,128)(2,1)S(1)} copy-done((bf16[16,100,1600]{2,0,1:T(8,128)(2,1)S(1)}, bf16[16,100,1600]{2,0,1:T(8,128)(2,1)}, u32[]{:S(2)}) %copy-start.1) | copy-done | bytes 5120024
  6.8 2.4 %vector_factor.1.own = bf16[100,16,200]{2,1,0:T(8,128)(2,1)S(1)} custom-call(bf16[112,200]{1,0:T(8,128)(2,1)S(1)} %get-tuple-element.48.after, bf16[1600,200]{1,0:T(8,128)(2,1)S(1)} %copy.13.trial, bf16[100,16,1600]{2,1,0:T(8,128)(2,1)S(1)} %bitcast.19), custom_call_target="tpu_custom_call" | custom-call | flops 1024000000 | bytes 8000000 | tf_op jit(solution)/shard_map/vector_factor/pallas_call | solution.py:360
  9.2 0.8 collective-permute-start.4
  9.9 1.6 collective-permute-start
  11.6 6.9 %collective-permute-start.5 = (bf16[100,200]{1,0:T(8,128)(2,1)S(1)}, bf16[100,200]{1,0:T(8,128)(2,1)S(1)}, u32[]{:S(2)}, u32[]{:S(2)}) collective-permute-start(bf16[100,200]{1,0:T(8,128)(2,1)S(1)} %bitcast.23), channel_id=1, source_target_pairs={{0,0},{1,1},{2,2},{3,3},{4,16},{5,17},{6,18},{7,19},{8,32},{9,33},... | collective-permute-start | bytes 120008 | tf_op jit(solution)/shard_map/ppermute | solution.py:62
  19.0 1.6 collective-permute-done.5.walker
  20.6 1.0 collective-permute-start.6
  21.6 2.6 %collective-permute-start.1 = (bf16[2,112,200]{2,1,0:T(8,128)(2,1)S(1)}, bf16[2,112,200]{2,1,0:T(8,128)(2,1)S(1)}, u32[]{:S(2)}, u32[]{:S(2)}) collective-permute-start(bf16[2,112,200]{2,1,0:T(8,128)(2,1)S(1)} %maximum_select_fusion.r0), channel_id=1, source_target_pairs={{0,192},{16,208},{32,224},{48,240},{64,0},{80,16},{96,32},{112,48}... | collective-permute-start | bytes 268808 | tf_op jit(solution)/shard_map/ppermute | solution.py:33
  26.5 2.6 %collective-permute-done.1.r1 = bf16[2,112,200]{2,1,0:T(8,128)(2,1)S(1)} collective-permute-done((bf16[2,112,200]{2,1,0:T(8,128)(2,1)S(1)}, bf16[2,112,200]{2,1,0:T(8,128)(2,1)S(1)}, u32[]{:S(2)}, u32[]{:S(2)}) %collective-permute-start.1) | collective-permute-done | bytes 89632 | tf_op jit(solution)/shard_map/ppermute | solution.py:33
  29.1 1.1 collective-permute-done.2.r2
  30.2 3.1 %collective-permute-done.3.r3 = bf16[2,112,200]{2,1,0:T(8,128)(2,1)S(1)} collective-permute-done((bf16[2,112,200]{2,1,0:T(8,128)(2,1)S(1)}, bf16[2,112,200]{2,1,0:T(8,128)(2,1)S(1)}, u32[]{:S(2)}, u32[]{:S(2)}) %collective-permute-start.3) | collective-permute-done | bytes 89632 | tf_op jit(solution)/shard_map/ppermute | solution.py:33
  33.2 1.5 force_bias.1
  34.7 2.9 %collective-permute-start.7 = (f32[8,32]{1,0:T(8,128)S(1)}, f32[8,32]{1,0:T(8,128)S(1)}, u32[]{:S(2)}, u32[]{:S(2)}) collective-permute-start(f32[8,32]{1,0:T(8,128)S(1)} %get-tuple-element.22), channel_id=1, source_target_pairs={{0,2},{1,3},{2,0},{3,1},{4,6},{5,7},{6,4},{7,5},{8,10},{9,11},{10,... | collective-permute-start | bytes 3080 | tf_op jit(solution)/shard_map/ppermute | solution.py:45
  38.1 2.3 %collective-permute-start.9 = (f32[8,32]{1,0:T(8,128)S(1)}, f32[8,32]{1,0:T(8,128)S(1)}, u32[]{:S(2)}, u32[]{:S(2)}) collective-permute-start(f32[8,32]{1,0:T(8,128)S(1)} %get-tuple-element.22), channel_id=1, source_target_pairs={{0,3},{1,0},{2,1},{3,2},{4,7},{5,4},{6,5},{7,6},{8,11},{9,8},{10,9... | collective-permute-start | bytes 3080 | tf_op jit(solution)/shard_map/ppermute | solution.py:45
  40.4 0.9 collective-permute-done.8
  41.4 5.0 %collective-permute-start.11 = (f32[8,32]{1,0:T(8,128)S(1)}, f32[8,32]{1,0:T(8,128)S(1)}, u32[]{:S(2)}, u32[]{:S(2)}) collective-permute-start(f32[8,32]{1,0:T(8,128)S(1)} %add_add_fusion.b0), channel_id=1, source_target_pairs={{0,8},{1,9},{2,10},{3,11},{4,12},{5,13},{6,14},{7,15},{8,0},{9,1},... | collective-permute-start | bytes 3080 | tf_op jit(solution)/shard_map/ppermute | solution.py:49
  46.5 2.9 %collective-permute-start.12 = (f32[8,32]{1,0:T(8,128)S(1)}, f32[8,32]{1,0:T(8,128)S(1)}, u32[]{:S(2)}, u32[]{:S(2)}) collective-permute-start(f32[8,32]{1,0:T(8,128)S(1)} %add_add_fusion.b0), channel_id=1, source_target_pairs={{0,12},{1,13},{2,14},{3,15},{4,0},{5,1},{6,2},{7,3},{8,4},{9,5},{1... | collective-permute-start | bytes 3080 | tf_op jit(solution)/shard_map/ppermute | solution.py:49
  49.5 0.7 collective-permute-done.12.b3
  50.2 2.5 %copy-done.2 = bf16[16,100,1600]{2,0,1:T(8,128)(2,1)S(1)} copy-done((bf16[16,100,1600]{2,0,1:T(8,128)(2,1)S(1)}, bf16[16,100,1600]{2,0,1:T(8,128)(2,1)}, u32[]{:S(2)}) %copy-start.2) | copy-done | bytes 5120024
  52.7 5.1 %operator_away.1 = (f32[8,32]{1,0:T(8,128)S(1)}, bf16[200,1600]{1,0:T(8,128)(2,1)S(1)}, bf16[200,1600]{1,0:T(8,128)(2,1)S(1)}) custom-call(s32[1]{0:T(128)} %bitcast.2.at, f32[8,32]{1,0:T(8,128)S(1)} %add_add_fusion.b0, f32[8,32]{1,0:T(8,128)S(1)} %collective-permute-done.10.b1, f32[8,32]{1,0:T(8,128)S(1)} %collective-permute-done.11.b2, ...), custom_call_target="tpu_custom_call" | custom-call | tf_op jit(solution)/shard_map/operator_away/pallas_call | solution.py:327
  57.8 1.0 collective-permute-start.20
  58.8 5.1 %operator_keep.1 = (bf16[100,1600]{1,0:T(8,128)(2,1)S(1)}, bf16[100,1600]{1,0:T(8,128)(2,1)S(1)}, bf16[100,1600]{1,0:T(8,128)(2,1)S(1)}, bf16[100,1600]{1,0:T(8,...) custom-call(s32[1]{0:T(128)} %bitcast.2.at, f32[8,32]{1,0:T(8,128)S(1)} %get-tuple-element.24.fields, ...), custom_call_target="tpu_custom_call" | custom-call | tf_op jit(solution)/shard_map/operator_keep/pallas_call | solution.py:327
  64.0 0.9 collective-permute-start.17
  64.8 1.8 %collective-permute-start.18 = (bf16[100,1600]{1,0:T(8,128)(2,1)S(1)}, bf16[100,1600]{1,0:T(8,128)(2,1)S(1)}, u32[]{:S(2)}, u32[]{:S(2)}) collective-permute-start(bf16[100,1600]{1,0:T(8,128)(2,1)S(1)} %get-tuple-element.29), channel_id=1, source_target_pairs={{0,192},{16,208},{32,224},{48,240},{64,0},{80,16},{96,32},{112,48}... | collective-permute-start | bytes 960008 | tf_op jit(solution)/shard_map/ppermute | solution.py:33
  66.7 9.8 %collective-permute-done.16.p1 = bf16[100,1600]{1,0:T(8,128)(2,1)S(1)} collective-permute-done((bf16[100,1600]{1,0:T(8,128)(2,1)S(1)}, bf16[100,1600]{1,0:T(8,128)(2,1)S(1)}, u32[]{:S(2)}, u32[]{:S(2)}) %collective-permute-start.16) | collective-permute-done | bytes 320032 | tf_op jit(solution)/shard_map/ppermute | solution.py:33
  76.5 1.6 collective-permute-start.25
  78.0 1.0 collective-permute-start.26
  79.0 2.0 %collective-permute-done.18.p3 = bf16[100,1600]{1,0:T(8,128)(2,1)S(1)} collective-permute-done((bf16[100,1600]{1,0:T(8,128)(2,1)S(1)}, bf16[100,1600]{1,0:T(8,128)(2,1)S(1)}, u32[]{:S(2)}, u32[]{:S(2)}) %collective-permute-start.18) | collective-permute-done | bytes 320032 | tf_op jit(solution)/shard_map/ppermute | solution.py:33
  81.2 1.0 collective-permute-start.19
  82.2 0.9 pair_sum.1
  83.8 3.9 %collective-permute-start.22 = (bf16[50,1600]{1,0:T(8,128)(2,1)}, bf16[50,1600]{1,0:T(8,128)(2,1)S(1)}, u32[]{:S(2)}, u32[]{:S(2)}) collective-permute-start(bf16[50,1600]{1,0:T(8,128)(2,1)} %get-tuple-element.34), channel_id=1, source_target_pairs={{0,128},{16,144},{32,160},{48,176},{64,192},{80,208},{96,224},{112... | collective-permute-start | bytes 480008 | tf_op jit(solution)/shard_map/ppermute | solution.py:33
  87.8 2.2 %collective-permute-done.21.q1 = bf16[50,1600]{1,0:T(8,128)(2,1)S(1)} collective-permute-done((bf16[50,1600]{1,0:T(8,128)(2,1)}, bf16[50,1600]{1,0:T(8,128)(2,1)S(1)}, u32[]{:S(2)}, u32[]{:S(2)}) %collective-permute-start.21) | collective-permute-done | bytes 160032 | tf_op jit(solution)/shard_map/ppermute | solution.py:33
  90.0 5.4 %collective-permute-done.22.q2 = bf16[50,1600]{1,0:T(8,128)(2,1)S(1)} collective-permute-done((bf16[50,1600]{1,0:T(8,128)(2,1)}, bf16[50,1600]{1,0:T(8,128)(2,1)S(1)}, u32[]{:S(2)}, u32[]{:S(2)}) %collective-permute-start.22) | collective-permute-done | bytes 160032 | tf_op jit(solution)/shard_map/ppermute | solution.py:33
  95.3 0.8 last_sum.1
  96.1 6.7 %collective-permute-start.27 = (bf16[50,1600]{1,0:T(8,128)(2,1)S(1)}, bf16[50,1600]{1,0:T(8,128)(2,1)S(1)}, u32[]{:S(2)}, u32[]{:S(2)}) collective-permute-start(bf16[50,1600]{1,0:T(8,128)(2,1)S(1)} %get-tuple-element.38), channel_id=1, source_target_pairs={{0,8},{1,9},{2,10},{3,11},{4,16},{5,17},{6,18},{7,19},{8,0},{9,1},... | collective-permute-start | bytes 480008 | tf_op jit(solution)/shard_map/ppermute | solution.py:62
  102.9 1.9 %collective-permute-start.28 = (bf16[50,1600]{1,0:T(8,128)(2,1)S(1)}, bf16[50,1600]{1,0:T(8,128)(2,1)S(1)}, u32[]{:S(2)}, u32[]{:S(2)}) collective-permute-start(bf16[50,1600]{1,0:T(8,128)(2,1)S(1)} %get-tuple-element.37.second), channel_id=1, source_target_pairs={{4,24},{5,25},{6,26},{7,27},{12,16},{13,17},{14,18},{15,19},{16,4}... | collective-permute-start | bytes 480008 | tf_op jit(solution)/shard_map/ppermute | solution.py:62
  104.8 5.4 %collective-permute-done.27.got = bf16[50,1600]{1,0:T(8,128)(2,1)S(1)} collective-permute-done((bf16[50,1600]{1,0:T(8,128)(2,1)S(1)}, bf16[50,1600]{1,0:T(8,128)(2,1)S(1)}, u32[]{:S(2)}, u32[]{:S(2)}) %collective-permute-start.27) | collective-permute-done | bytes 160032 | tf_op jit(solution)/shard_map/ppermute | solution.py:62
  110.2 3.1 %collective-permute-done.28.more = bf16[50,1600]{1,0:T(8,128)(2,1)S(1)} collective-permute-done((bf16[50,1600]{1,0:T(8,128)(2,1)S(1)}, bf16[50,1600]{1,0:T(8,128)(2,1)S(1)}, u32[]{:S(2)}, u32[]{:S(2)}) %collective-permute-start.28) | collective-permute-done | bytes 160032 | tf_op jit(solution)/shard_map/ppermute | solution.py:62
  113.8 2.5 %collective-permute-start.29 = (bf16[50,1600]{1,0:T(8,128)(2,1)S(1)}, bf16[50,1600]{1,0:T(8,128)(2,1)S(1)}, u32[]{:S(2)}, u32[]{:S(2)}) collective-permute-start(bf16[50,1600]{1,0:T(8,128)(2,1)S(1)} %get-tuple-element.39.refs_0_), channel_id=1, source_target_pairs={{0,32},{16,48},{32,0},{48,16},{64,96},{80,112},{96,64},{112,80},{1... | collective-permute-start | bytes 480008 | tf_op jit(solution)/shard_map/ppermute | solution.py:37
  116.7 2.8 %collective-permute-start.34 = (bf16[50,1600]{1,0:T(8,128)(2,1)S(1)}, bf16[50,1600]{1,0:T(8,128)(2,1)S(1)}, u32[]{:S(2)}, u32[]{:S(2)}) collective-permute-start(bf16[50,1600]{1,0:T(8,128)(2,1)S(1)} %get-tuple-element.40.refs_0_), channel_id=1, source_target_pairs={{0,2},{1,3},{2,0},{3,1},{4,6},{5,7},{6,4},{7,5},{8,10},{9,11},{10,... | collective-permute-start | bytes 480008 | tf_op jit(solution)/shard_map/ppermute | solution.py:45
  119.5 1.4 collective-permute-start.35
  121.3 3.4 %collective-permute-done.33.refs_1_ = bf16[50,1600]{1,0:T(8,128)(2,1)S(1)} collective-permute-done((bf16[50,1600]{1,0:T(8,128)(2,1)S(1)}, bf16[50,1600]{1,0:T(8,128)(2,1)S(1)}, u32[]{:S(2)}, u32[]{:S(2)}) %collective-permute-start.33) | collective-permute-done | bytes 160032 | tf_op jit(solution)/shard_map/ppermute | solution.py:45
  124.7 1.6 collective-permute-done.34.refs_2_
  126.3 0.9 collective-permute-done.35.refs_3_
  127.3 1.6 collective-permute-start.36
  129.5 1.0 collective-permute-start.44
  130.5 3.1 %collective-permute-start.31 = (bf16[100,1600]{1,0:T(8,128)(2,1)S(1)}, bf16[100,1600]{1,0:T(8,128)(2,1)}, u32[]{:S(2)}, u32[]{:S(2)}) collective-permute-start(bf16[100,1600]{1,0:T(8,128)(2,1)S(1)} %stack_low.1.refs_4_.refs_0_), channel_id=1, source_target_pairs={{0,2},{1,3},{2,0},{3,1},{4,6},{5,7},{6,4},{7,5},{8,10},{9,11},{10,... | collective-permute-start | bytes 960008 | tf_op jit(solution)/shard_map/ppermute | solution.py:45
  133.9 5.0 %collective-permute-done.30.refs_1_ = bf16[100,1600]{1,0:T(8,128)(2,1)S(1)} collective-permute-done((bf16[100,1600]{1,0:T(8,128)(2,1)S(1)}, bf16[100,1600]{1,0:T(8,128)(2,1)S(1)}, u32[]{:S(2)}, u32[]{:S(2)}) %collective-permute-start.30) | collective-permute-done | bytes 320032 | tf_op jit(solution)/shard_map/ppermute | solution.py:45
  138.9 2.0 %collective-permute-start.41 = (bf16[200,1600]{1,0:T(8,128)(2,1)S(1)}, bf16[200,1600]{1,0:T(8,128)(2,1)S(1)}, u32[]{:S(2)}, u32[]{:S(2)}) collective-permute-start(bf16[200,1600]{1,0:T(8,128)(2,1)S(1)} %stack_y.1.refs_4_), channel_id=1, source_target_pairs={{0,16},{16,0},{32,48},{48,32},{64,80},{80,64},{96,112},{112,96},{1... | collective-permute-start | bytes 1920008 | tf_op jit(solution)/shard_map/ppermute | solution.py:41
  140.8 3.0 %collective-permute-done.36.refs_5_ = bf16[200,1600]{1,0:T(8,128)(2,1)S(1)} collective-permute-done((bf16[200,1600]{1,0:T(8,128)(2,1)S(1)}, bf16[200,1600]{1,0:T(8,128)(2,1)S(1)}, u32[]{:S(2)}, u32[]{:S(2)}) %collective-permute-start.36) | collective-permute-done | bytes 640032 | tf_op jit(solution)/shard_map/ppermute | solution.py:37
  143.8 1.0 collective-permute-start.42
  144.8 2.7 %collective-permute-done.31.refs_2_ = bf16[100,1600]{1,0:T(8,128)(2,1)} collective-permute-done((bf16[100,1600]{1,0:T(8,128)(2,1)S(1)}, bf16[100,1600]{1,0:T(8,128)(2,1)}, u32[]{:S(2)}, u32[]{:S(2)}) %collective-permute-start.31) | collective-permute-done | bytes 320032 | tf_op jit(solution)/shard_map/ppermute | solution.py:45
  147.6 1.5 collective-permute-start.38
  149.2 0.8 collective-permute-start.39
  150.7 0.9 collective-permute-done.39.refs_8_
  152.1 0.9 copy-done.4
  153.1 13.6 %taylor.1 = bf16[100,200]{1,0:T(8,128)(2,1)S(1)} custom-call(s32[4]{0:T(128)S(1)} %pad_add_fusion.at, bf16[100,1600]{1,0:T(8,128)(2,1)S(1)} %stack_low.1.refs_4_.refs_0_, bf16[100,1600]{1,0:T(8,128)(2,1)S(1)} %collective-permute-done.30.refs_1_, bf16[100,1600]{1,0:T(8,128)(2,1)} %collective-permute-done.31.refs_2_, ...), custom_call_target="tpu_custom_call" | custom-call | tf_op jit(solution)/shard_map/taylor/pallas_call | solution.py:327
  166.6 1.9 %collective-permute-start.43 = (bf16[100,200]{1,0:T(8,128)(2,1)S(1)}, bf16[100,200]{1,0:T(8,128)(2,1)S(1)}, u32[]{:S(2)}, u32[]{:S(2)}) collective-permute-start(bf16[100,200]{1,0:T(8,128)(2,1)S(1)} %taylor.1), channel_id=1, source_target_pairs={{0,0},{1,1},{2,2},{3,3},{4,16},{5,17},{6,18},{7,19},{8,32},{9,33},... | collective-permute-start | bytes 120008 | tf_op jit(solution)/shard_map/ppermute | solution.py:62
  168.6 0.7 broadcast_select_fusion
  169.2 6.2 %collective-permute-done.43 = bf16[100,200]{1,0:T(8,128)(2,1)S(1)} collective-permute-done((bf16[100,200]{1,0:T(8,128)(2,1)S(1)}, bf16[100,200]{1,0:T(8,128)(2,1)S(1)}, u32[]{:S(2)}, u32[]{:S(2)}) %collective-permute-start.43) | collective-permute-done | bytes 40032 | tf_op jit(solution)/shard_map/ppermute | solution.py:62
  175.4 0.7 copy.14
  (74 shorter events, 8.4 us)
Async XLA Ops:
  0.6 0.9 copy-start
  0.6 10.9 %copy-start.5 = (bf16[1,100,200]{1,2,0:T(8,128)(2,1)S(1)}, bf16[1,100,200]{1,2,0:T(8,128)(2,1)}, u32[]{:S(2)}) copy-start(bf16[1,100,200]{1,2,0:T(8,128)(2,1)} %param.8) | copy-start | bytes 120004
  0.7 17.9 %copy-start.6 = (f32[16,16]{1,0:T(8,128)S(1)}, f32[16,16]{1,0:T(8,128)}, u32[]{:S(2)}) copy-start(f32[16,16]{1,0:T(8,128)} %param.11) | copy-start | bytes 3076
  0.7 49.5 %collective-permute-start.14 = (bf16[100,16,1600]{2,1,0:T(8,128)(2,1)}, bf16[100,16,1600]{2,1,0:T(8,128)(2,1)}, u32[]{:S(2)}, u32[]{:S(2)}) collective-permute-start(bf16[100,16,1600]{2,1,0:T(8,128)(2,1)} %bitcast.18), channel_id=1, source_target_pairs={{0,16},{16,0},{32,48},{48,32},{64,80},{80,64},{96,112},{112,96},{1... | collective-permute-start | bytes 15360008 | tf_op jit(solution)/shard_map/ppermute | solution.py:41
  4.3 2.5 %copy-start.1 = (bf16[16,100,1600]{2,0,1:T(8,128)(2,1)S(1)}, bf16[16,100,1600]{2,0,1:T(8,128)(2,1)}, u32[]{:S(2)}) copy-start(bf16[16,100,1600]{2,0,1:T(8,128)(2,1)} %param.7) | copy-start | bytes 15360004
  9.2 24.1 %collective-permute-start.4 = (bf16[100,16,200]{2,1,0:T(8,128)(2,1)S(1)}, bf16[100,16,200]{2,1,0:T(8,128)(2,1)S(1)}, u32[]{:S(2)}, u32[]{:S(2)}) collective-permute-start(bf16[100,16,200]{2,1,0:T(8,128)(2,1)S(1)} %vector_factor.1.own), channel_id=1, source_target_pairs={{0,16},{16,0},{32,48},{48,32},{64,80},{80,64},{96,112},{112,96},{1... | collective-permute-start | bytes 1920008 | tf_op jit(solution)/shard_map/ppermute | solution.py:41
  9.9 11.7 %collective-permute-start = (bf16[112,200]{1,0:T(8,128)(2,1)S(1)}, bf16[112,200]{1,0:T(8,128)(2,1)S(1)}, u32[]{:S(2)}, u32[]{:S(2)}) collective-permute-start(bf16[112,200]{1,0:T(8,128)(2,1)S(1)} %get-tuple-element.48.after), channel_id=1, source_target_pairs={{0,32},{16,48},{32,0},{48,16},{64,96},{80,112},{96,64},{112,80},{1... | collective-permute-start | bytes 134408 | tf_op jit(solution)/shard_map/ppermute | solution.py:37
  11.6 9.0 %collective-permute-start.5 = (bf16[100,200]{1,0:T(8,128)(2,1)S(1)}, bf16[100,200]{1,0:T(8,128)(2,1)S(1)}, u32[]{:S(2)}, u32[]{:S(2)}) collective-permute-start(bf16[100,200]{1,0:T(8,128)(2,1)S(1)} %bitcast.23), channel_id=1, source_target_pairs={{0,0},{1,1},{2,2},{3,3},{4,16},{5,17},{6,18},{7,19},{8,32},{9,33},... | collective-permute-start | bytes 120008 | tf_op jit(solution)/shard_map/ppermute | solution.py:62
  18.5 5.7 %collective-permute-start.13 = (f32[16,16]{1,0:T(8,128)S(1)}, f32[16,16]{1,0:T(8,128)S(1)}, u32[]{:S(2)}, u32[]{:S(2)}) collective-permute-start(f32[16,16]{1,0:T(8,128)S(1)} %copy-done.6), channel_id=1, source_target_pairs={{0,16},{16,0},{32,48},{48,32},{64,80},{80,64},{96,112},{112,96},{1... | collective-permute-start | bytes 3080 | tf_op jit(solution)/shard_map/ppermute | solution.py:41
  20.6 4.1 %collective-permute-start.6 = (bf16[100,200]{1,0:T(8,128)(2,1)S(1)}, bf16[100,200]{1,0:T(8,128)(2,1)S(1)}, u32[]{:S(2)}, u32[]{:S(2)}) collective-permute-start(bf16[100,200]{1,0:T(8,128)(2,1)S(1)} %collective-permute-done.5.walker), channel_id=1, source_target_pairs={{0,16},{16,0},{32,48},{48,32},{64,80},{80,64},{96,112},{112,96},{1... | collective-permute-start | bytes 120008 | tf_op jit(solution)/shard_map/ppermute | solution.py:41
  21.6 7.4 %collective-permute-start.1 = (bf16[2,112,200]{2,1,0:T(8,128)(2,1)S(1)}, bf16[2,112,200]{2,1,0:T(8,128)(2,1)S(1)}, u32[]{:S(2)}, u32[]{:S(2)}) collective-permute-start(bf16[2,112,200]{2,1,0:T(8,128)(2,1)S(1)} %maximum_select_fusion.r0), channel_id=1, source_target_pairs={{0,192},{16,208},{32,224},{48,240},{64,0},{80,16},{96,32},{112,48}... | collective-permute-start | bytes 268808 | tf_op jit(solution)/shard_map/ppermute | solution.py:33
  24.2 6.0 %collective-permute-start.2 = (bf16[2,112,200]{2,1,0:T(8,128)(2,1)S(1)}, bf16[2,112,200]{2,1,0:T(8,128)(2,1)S(1)}, u32[]{:S(2)}, u32[]{:S(2)}) collective-permute-start(bf16[2,112,200]{2,1,0:T(8,128)(2,1)S(1)} %maximum_select_fusion.r0), channel_id=1, source_target_pairs={{0,128},{16,144},{32,160},{48,176},{64,192},{80,208},{96,224},{112... | collective-permute-start | bytes 268808 | tf_op jit(solution)/shard_map/ppermute | solution.py:33
  24.7 8.5 %collective-permute-start.3 = (bf16[2,112,200]{2,1,0:T(8,128)(2,1)S(1)}, bf16[2,112,200]{2,1,0:T(8,128)(2,1)S(1)}, u32[]{:S(2)}, u32[]{:S(2)}) collective-permute-start(bf16[2,112,200]{2,1,0:T(8,128)(2,1)S(1)} %maximum_select_fusion.r0), channel_id=1, source_target_pairs={{0,64},{16,80},{32,96},{48,112},{64,128},{80,144},{96,160},{112,17... | collective-permute-start | bytes 268808 | tf_op jit(solution)/shard_map/ppermute | solution.py:33
  34.7 5.7 %collective-permute-start.7 = (f32[8,32]{1,0:T(8,128)S(1)}, f32[8,32]{1,0:T(8,128)S(1)}, u32[]{:S(2)}, u32[]{:S(2)}) collective-permute-start(f32[8,32]{1,0:T(8,128)S(1)} %get-tuple-element.22), channel_id=1, source_target_pairs={{0,2},{1,3},{2,0},{3,1},{4,6},{5,7},{6,4},{7,5},{8,10},{9,11},{10,... | collective-permute-start | bytes 3080 | tf_op jit(solution)/shard_map/ppermute | solution.py:45
  37.7 3.7 %collective-permute-start.8 = (f32[8,32]{1,0:T(8,128)S(1)}, f32[8,32]{1,0:T(8,128)S(1)}, u32[]{:S(2)}, u32[]{:S(2)}) collective-permute-start(f32[8,32]{1,0:T(8,128)S(1)} %get-tuple-element.22), channel_id=1, source_target_pairs={{0,1},{1,2},{2,3},{3,0},{4,5},{5,6},{6,7},{7,4},{8,9},{9,10},{10,1... | collective-permute-start | bytes 3080 | tf_op jit(solution)/shard_map/ppermute | solution.py:45
  38.1 3.3 %collective-permute-start.9 = (f32[8,32]{1,0:T(8,128)S(1)}, f32[8,32]{1,0:T(8,128)S(1)}, u32[]{:S(2)}, u32[]{:S(2)}) collective-permute-start(f32[8,32]{1,0:T(8,128)S(1)} %get-tuple-element.22), channel_id=1, source_target_pairs={{0,3},{1,0},{2,1},{3,2},{4,7},{5,4},{6,5},{7,6},{8,11},{9,8},{10,9... | collective-permute-start | bytes 3080 | tf_op jit(solution)/shard_map/ppermute | solution.py:45
  40.4 9.8 %collective-permute-start.15 = (bf16[200,200]{1,0:T(8,128)(2,1)S(1)}, bf16[200,200]{1,0:T(8,128)(2,1)S(1)}, u32[]{:S(2)}, u32[]{:S(2)}) collective-permute-start(bf16[200,200]{1,0:T(8,128)(2,1)S(1)} %get-tuple-element.23.walkers), channel_id=1, source_target_pairs={{0,32},{16,48},{32,0},{48,16},{64,96},{80,112},{96,64},{112,80},{1... | collective-permute-start | bytes 240008 | tf_op jit(solution)/shard_map/ppermute | solution.py:37
  41.4 8.2 %collective-permute-start.10 = (f32[8,32]{1,0:T(8,128)S(1)}, f32[8,32]{1,0:T(8,128)S(1)}, u32[]{:S(2)}, u32[]{:S(2)}) collective-permute-start(f32[8,32]{1,0:T(8,128)S(1)} %add_add_fusion.b0), channel_id=1, source_target_pairs={{0,4},{1,5},{2,6},{3,7},{4,8},{5,9},{6,10},{7,11},{8,12},{9,13},{1... | collective-permute-start | bytes 3080 | tf_op jit(solution)/shard_map/ppermute | solution.py:49
  41.4 8.1 %collective-permute-start.11 = (f32[8,32]{1,0:T(8,128)S(1)}, f32[8,32]{1,0:T(8,128)S(1)}, u32[]{:S(2)}, u32[]{:S(2)}) collective-permute-start(f32[8,32]{1,0:T(8,128)S(1)} %add_add_fusion.b0), channel_id=1, source_target_pairs={{0,8},{1,9},{2,10},{3,11},{4,12},{5,13},{6,14},{7,15},{8,0},{9,1},... | collective-permute-start | bytes 3080 | tf_op jit(solution)/shard_map/ppermute | solution.py:49
  46.5 3.7 %collective-permute-start.12 = (f32[8,32]{1,0:T(8,128)S(1)}, f32[8,32]{1,0:T(8,128)S(1)}, u32[]{:S(2)}, u32[]{:S(2)}) collective-permute-start(f32[8,32]{1,0:T(8,128)S(1)} %add_add_fusion.b0), channel_id=1, source_target_pairs={{0,12},{1,13},{2,14},{3,15},{4,0},{5,1},{6,2},{7,3},{8,4},{9,5},{1... | collective-permute-start | bytes 3080 | tf_op jit(solution)/shard_map/ppermute | solution.py:49
  50.2 2.5 %copy-start.2 = (bf16[16,100,1600]{2,0,1:T(8,128)(2,1)S(1)}, bf16[16,100,1600]{2,0,1:T(8,128)(2,1)}, u32[]{:S(2)}) copy-start(bf16[16,100,1600]{2,0,1:T(8,128)(2,1)} %param.7) | copy-start | bytes 15360004
  57.8 24.4 %collective-permute-start.20 = (bf16[200,1600]{1,0:T(8,128)(2,1)S(1)}, bf16[200,1600]{1,0:T(8,128)(2,1)S(1)}, u32[]{:S(2)}, u32[]{:S(2)}) collective-permute-start(bf16[200,1600]{1,0:T(8,128)(2,1)S(1)} %get-tuple-element.31), channel_id=1, source_target_pairs={{0,32},{16,48},{32,0},{48,16},{64,96},{80,112},{96,64},{112,80},{1... | collective-permute-start | bytes 1920008 | tf_op jit(solution)/shard_map/ppermute | solution.py:37
  63.9 63.3 %copy-start.3 = (bf16[400,200]{1,0:T(8,128)(2,1)}, bf16[400,200]{1,0:T(8,128)(2,1)S(1)}, u32[]{:S(2)}) copy-start(bf16[400,200]{1,0:T(8,128)(2,1)S(1)} %get-tuple-element.36.refs_12_) | copy-start | bytes 480004
  63.9 12.6 %collective-permute-start.16 = (bf16[100,1600]{1,0:T(8,128)(2,1)S(1)}, bf16[100,1600]{1,0:T(8,128)(2,1)S(1)}, u32[]{:S(2)}, u32[]{:S(2)}) collective-permute-start(bf16[100,1600]{1,0:T(8,128)(2,1)S(1)} %get-tuple-element.27), channel_id=1, source_target_pairs={{0,64},{16,80},{32,96},{48,112},{64,128},{80,144},{96,160},{112,17... | collective-permute-start | bytes 960008 | tf_op jit(solution)/shard_map/ppermute | solution.py:33
  64.0 14.0 %collective-permute-start.17 = (bf16[100,1600]{1,0:T(8,128)(2,1)S(1)}, bf16[100,1600]{1,0:T(8,128)(2,1)S(1)}, u32[]{:S(2)}, u32[]{:S(2)}) collective-permute-start(bf16[100,1600]{1,0:T(8,128)(2,1)S(1)} %get-tuple-element.28), channel_id=1, source_target_pairs={{0,128},{16,144},{32,160},{48,176},{64,192},{80,208},{96,224},{112... | collective-permute-start | bytes 960008 | tf_op jit(solution)/shard_map/ppermute | solution.py:33
  64.8 16.2 %collective-permute-start.18 = (bf16[100,1600]{1,0:T(8,128)(2,1)S(1)}, bf16[100,1600]{1,0:T(8,128)(2,1)S(1)}, u32[]{:S(2)}, u32[]{:S(2)}) collective-permute-start(bf16[100,1600]{1,0:T(8,128)(2,1)S(1)} %get-tuple-element.29), channel_id=1, source_target_pairs={{0,192},{16,208},{32,224},{48,240},{64,0},{80,16},{96,32},{112,48}... | collective-permute-start | bytes 960008 | tf_op jit(solution)/shard_map/ppermute | solution.py:33
  66.7 17.1 %collective-permute-start.24 = (bf16[400,200]{1,0:T(8,128)(2,1)S(1)}, bf16[400,200]{1,0:T(8,128)(2,1)S(1)}, u32[]{:S(2)}, u32[]{:S(2)}) collective-permute-start(bf16[400,200]{1,0:T(8,128)(2,1)S(1)} %get-tuple-element.36.refs_12_), channel_id=1, source_target_pairs={{0,1},{1,2},{2,3},{3,0},{4,5},{5,6},{6,7},{7,4},{8,9},{9,10},{10,1... | collective-permute-start | bytes 480008 | tf_op jit(solution)/shard_map/ppermute | solution.py:45
  76.5 11.2 %collective-permute-start.25 = (bf16[400,200]{1,0:T(8,128)(2,1)S(1)}, bf16[400,200]{1,0:T(8,128)(2,1)S(1)}, u32[]{:S(2)}, u32[]{:S(2)}) collective-permute-start(bf16[400,200]{1,0:T(8,128)(2,1)S(1)} %get-tuple-element.36.refs_12_), channel_id=1, source_target_pairs={{0,2},{1,3},{2,0},{3,1},{4,6},{5,7},{6,4},{7,5},{8,10},{9,11},{10,... | collective-permute-start | bytes 480008 | tf_op jit(solution)/shard_map/ppermute | solution.py:45
  78.0 9.8 %collective-permute-start.26 = (bf16[400,200]{1,0:T(8,128)(2,1)S(1)}, bf16[400,200]{1,0:T(8,128)(2,1)S(1)}, u32[]{:S(2)}, u32[]{:S(2)}) collective-permute-start(bf16[400,200]{1,0:T(8,128)(2,1)S(1)} %get-tuple-element.36.refs_12_), channel_id=1, source_target_pairs={{0,3},{1,0},{2,1},{3,2},{4,7},{5,4},{6,5},{7,6},{8,11},{9,8},{10,9... | collective-permute-start | bytes 480008 | tf_op jit(solution)/shard_map/ppermute | solution.py:45
  81.2 6.6 %collective-permute-start.19 = (bf16[50,1600]{1,0:T(8,128)(2,1)S(1)}, bf16[50,1600]{1,0:T(8,128)(2,1)S(1)}, u32[]{:S(2)}, u32[]{:S(2)}) collective-permute-start(bf16[50,1600]{1,0:T(8,128)(2,1)S(1)} %x_sum.1), channel_id=1, source_target_pairs={{0,32},{16,48},{32,0},{48,16},{64,96},{80,112},{96,64},{112,80},{1... | collective-permute-start | bytes 480008 | tf_op jit(solution)/shard_map/ppermute | solution.py:37
  83.1 6.9 %collective-permute-start.21 = (bf16[50,1600]{1,0:T(8,128)(2,1)}, bf16[50,1600]{1,0:T(8,128)(2,1)S(1)}, u32[]{:S(2)}, u32[]{:S(2)}) collective-permute-start(bf16[50,1600]{1,0:T(8,128)(2,1)} %get-tuple-element.33), channel_id=1, source_target_pairs={{0,64},{16,80},{32,96},{48,112},{64,128},{80,144},{96,160},{112,17... | collective-permute-start | bytes 480008 | tf_op jit(solution)/shard_map/ppermute | solution.py:33
  83.8 11.6 %collective-permute-start.22 = (bf16[50,1600]{1,0:T(8,128)(2,1)}, bf16[50,1600]{1,0:T(8,128)(2,1)S(1)}, u32[]{:S(2)}, u32[]{:S(2)}) collective-permute-start(bf16[50,1600]{1,0:T(8,128)(2,1)} %get-tuple-element.34), channel_id=1, source_target_pairs={{0,128},{16,144},{32,160},{48,176},{64,192},{80,208},{96,224},{112... | collective-permute-start | bytes 480008 | tf_op jit(solution)/shard_map/ppermute | solution.py:33
  87.7 7.6 %collective-permute-start.23 = (bf16[50,1600]{1,0:T(8,128)(2,1)}, bf16[50,1600]{1,0:T(8,128)(2,1)S(1)}, u32[]{:S(2)}, u32[]{:S(2)}) collective-permute-start(bf16[50,1600]{1,0:T(8,128)(2,1)} %get-tuple-element.35), channel_id=1, source_target_pairs={{0,192},{16,208},{32,224},{48,240},{64,0},{80,16},{96,32},{112,48}... | collective-permute-start | bytes 480008 | tf_op jit(solution)/shard_map/ppermute | solution.py:33
  96.1 14.1 %collective-permute-start.27 = (bf16[50,1600]{1,0:T(8,128)(2,1)S(1)}, bf16[50,1600]{1,0:T(8,128)(2,1)S(1)}, u32[]{:S(2)}, u32[]{:S(2)}) collective-permute-start(bf16[50,1600]{1,0:T(8,128)(2,1)S(1)} %get-tuple-element.38), channel_id=1, source_target_pairs={{0,8},{1,9},{2,10},{3,11},{4,16},{5,17},{6,18},{7,19},{8,0},{9,1},... | collective-permute-start | bytes 480008 | tf_op jit(solution)/shard_map/ppermute | solution.py:62
  102.9 10.4 %collective-permute-start.28 = (bf16[50,1600]{1,0:T(8,128)(2,1)S(1)}, bf16[50,1600]{1,0:T(8,128)(2,1)S(1)}, u32[]{:S(2)}, u32[]{:S(2)}) collective-permute-start(bf16[50,1600]{1,0:T(8,128)(2,1)S(1)} %get-tuple-element.37.second), channel_id=1, source_target_pairs={{4,24},{5,25},{6,26},{7,27},{12,16},{13,17},{14,18},{15,19},{16,4}... | collective-permute-start | bytes 480008 | tf_op jit(solution)/shard_map/ppermute | solution.py:62
  113.8 7.4 %collective-permute-start.29 = (bf16[50,1600]{1,0:T(8,128)(2,1)S(1)}, bf16[50,1600]{1,0:T(8,128)(2,1)S(1)}, u32[]{:S(2)}, u32[]{:S(2)}) collective-permute-start(bf16[50,1600]{1,0:T(8,128)(2,1)S(1)} %get-tuple-element.39.refs_0_), channel_id=1, source_target_pairs={{0,32},{16,48},{32,0},{48,16},{64,96},{80,112},{96,64},{112,80},{1... | collective-permute-start | bytes 480008 | tf_op jit(solution)/shard_map/ppermute | solution.py:37
  116.3 8.4 %collective-permute-start.33 = (bf16[50,1600]{1,0:T(8,128)(2,1)S(1)}, bf16[50,1600]{1,0:T(8,128)(2,1)S(1)}, u32[]{:S(2)}, u32[]{:S(2)}) collective-permute-start(bf16[50,1600]{1,0:T(8,128)(2,1)S(1)} %get-tuple-element.40.refs_0_), channel_id=1, source_target_pairs={{0,1},{1,2},{2,3},{3,0},{4,5},{5,6},{6,7},{7,4},{8,9},{9,10},{10,1... | collective-permute-start | bytes 480008 | tf_op jit(solution)/shard_map/ppermute | solution.py:45
  116.7 9.5 %collective-permute-start.34 = (bf16[50,1600]{1,0:T(8,128)(2,1)S(1)}, bf16[50,1600]{1,0:T(8,128)(2,1)S(1)}, u32[]{:S(2)}, u32[]{:S(2)}) collective-permute-start(bf16[50,1600]{1,0:T(8,128)(2,1)S(1)} %get-tuple-element.40.refs_0_), channel_id=1, source_target_pairs={{0,2},{1,3},{2,0},{3,1},{4,6},{5,7},{6,4},{7,5},{8,10},{9,11},{10,... | collective-permute-start | bytes 480008 | tf_op jit(solution)/shard_map/ppermute | solution.py:45
  119.5 7.6 %collective-permute-start.35 = (bf16[50,1600]{1,0:T(8,128)(2,1)S(1)}, bf16[50,1600]{1,0:T(8,128)(2,1)S(1)}, u32[]{:S(2)}, u32[]{:S(2)}) collective-permute-start(bf16[50,1600]{1,0:T(8,128)(2,1)S(1)} %get-tuple-element.40.refs_0_), channel_id=1, source_target_pairs={{0,3},{1,0},{2,1},{3,2},{4,7},{5,4},{6,5},{7,6},{8,11},{9,8},{10,9... | collective-permute-start | bytes 480008 | tf_op jit(solution)/shard_map/ppermute | solution.py:45
  127.3 16.5 %collective-permute-start.36 = (bf16[200,1600]{1,0:T(8,128)(2,1)S(1)}, bf16[200,1600]{1,0:T(8,128)(2,1)S(1)}, u32[]{:S(2)}, u32[]{:S(2)}) collective-permute-start(bf16[200,1600]{1,0:T(8,128)(2,1)S(1)} %stack_y.1.refs_4_), channel_id=1, source_target_pairs={{0,32},{16,48},{32,0},{48,16},{64,96},{80,112},{96,64},{112,80},{1... | collective-permute-start | bytes 1920008 | tf_op jit(solution)/shard_map/ppermute | solution.py:37
  128.9 10.0 %collective-permute-start.30 = (bf16[100,1600]{1,0:T(8,128)(2,1)S(1)}, bf16[100,1600]{1,0:T(8,128)(2,1)S(1)}, u32[]{:S(2)}, u32[]{:S(2)}) collective-permute-start(bf16[100,1600]{1,0:T(8,128)(2,1)S(1)} %stack_low.1.refs_4_.refs_0_), channel_id=1, source_target_pairs={{0,1},{1,2},{2,3},{3,0},{4,5},{5,6},{6,7},{7,4},{8,9},{9,10},{10,1... | collective-permute-start | bytes 960008 | tf_op jit(solution)/shard_map/ppermute | solution.py:45
  129.5 4.1 %collective-permute-start.44 = (f32[8,16]{1,0:T(8,128)S(1)}, f32[8,16]{1,0:T(8,128)S(1)}, u32[]{:S(2)}, u32[]{:S(2)}) collective-permute-start(f32[8,16]{1,0:T(8,128)S(1)} %get-tuple-element.50), channel_id=1, source_target_pairs={{0,16},{16,0},{32,48},{48,32},{64,80},{80,64},{96,112},{112,96},{1... | collective-permute-start | bytes 1544 | tf_op jit(solution)/shard_map/ppermute | solution.py:41
  130.5 17.1 %collective-permute-start.31 = (bf16[100,1600]{1,0:T(8,128)(2,1)S(1)}, bf16[100,1600]{1,0:T(8,128)(2,1)}, u32[]{:S(2)}, u32[]{:S(2)}) collective-permute-start(bf16[100,1600]{1,0:T(8,128)(2,1)S(1)} %stack_low.1.refs_4_.refs_0_), channel_id=1, source_target_pairs={{0,2},{1,3},{2,0},{3,1},{4,6},{5,7},{6,4},{7,5},{8,10},{9,11},{10,... | collective-permute-start | bytes 960008 | tf_op jit(solution)/shard_map/ppermute | solution.py:45
  133.6 15.6 %collective-permute-start.32 = (bf16[100,1600]{1,0:T(8,128)(2,1)S(1)}, bf16[100,1600]{1,0:T(8,128)(2,1)}, u32[]{:S(2)}, u32[]{:S(2)}) collective-permute-start(bf16[100,1600]{1,0:T(8,128)(2,1)S(1)} %stack_low.1.refs_4_.refs_0_), channel_id=1, source_target_pairs={{0,3},{1,0},{2,1},{3,2},{4,7},{5,4},{6,5},{7,6},{8,11},{9,8},{10,9... | collective-permute-start | bytes 960008 | tf_op jit(solution)/shard_map/ppermute | solution.py:45
  133.6 16.4 %collective-permute-start.37 = (bf16[100,1600]{1,0:T(8,128)(2,1)S(1)}, bf16[100,1600]{1,0:T(8,128)(2,1)}, u32[]{:S(2)}, u32[]{:S(2)}) collective-permute-start(bf16[100,1600]{1,0:T(8,128)(2,1)S(1)} %stack_low.1.refs_4_.refs_0_), channel_id=1, source_target_pairs={{0,16},{16,0},{32,48},{48,32},{64,80},{80,64},{96,112},{112,96},{1... | collective-permute-start | bytes 960008 | tf_op jit(solution)/shard_map/ppermute | solution.py:41
  138.9 11.8 %collective-permute-start.41 = (bf16[200,1600]{1,0:T(8,128)(2,1)S(1)}, bf16[200,1600]{1,0:T(8,128)(2,1)S(1)}, u32[]{:S(2)}, u32[]{:S(2)}) collective-permute-start(bf16[200,1600]{1,0:T(8,128)(2,1)S(1)} %stack_y.1.refs_4_), channel_id=1, source_target_pairs={{0,16},{16,0},{32,48},{48,32},{64,80},{80,64},{96,112},{112,96},{1... | collective-permute-start | bytes 1920008 | tf_op jit(solution)/shard_map/ppermute | solution.py:41
  143.8 8.4 %collective-permute-start.42 = (bf16[200,1600]{1,0:T(8,128)(2,1)S(1)}, bf16[200,1600]{1,0:T(8,128)(2,1)}, u32[]{:S(2)}, u32[]{:S(2)}) collective-permute-start(bf16[200,1600]{1,0:T(8,128)(2,1)S(1)} %collective-permute-done.36.refs_5_), channel_id=1, source_target_pairs={{0,16},{16,0},{32,48},{48,32},{64,80},{80,64},{96,112},{112,96},{1... | collective-permute-start | bytes 1920008 | tf_op jit(solution)/shard_map/ppermute | solution.py:41
  147.6 3.1 %collective-permute-start.38 = (bf16[100,1600]{1,0:T(8,128)(2,1)S(1)}, bf16[100,1600]{1,0:T(8,128)(2,1)}, u32[]{:S(2)}, u32[]{:S(2)}) collective-permute-start(bf16[100,1600]{1,0:T(8,128)(2,1)S(1)} %collective-permute-done.30.refs_1_), channel_id=1, source_target_pairs={{0,16},{16,0},{32,48},{48,32},{64,80},{80,64},{96,112},{112,96},{1... | collective-permute-start | bytes 960008 | tf_op jit(solution)/shard_map/ppermute | solution.py:41
  149.2 2.4 %collective-permute-start.39 = (bf16[100,1600]{1,0:T(8,128)(2,1)}, bf16[100,1600]{1,0:T(8,128)(2,1)}, u32[]{:S(2)}, u32[]{:S(2)}) collective-permute-start(bf16[100,1600]{1,0:T(8,128)(2,1)} %collective-permute-done.31.refs_2_), channel_id=1, source_target_pairs={{0,16},{16,0},{32,48},{48,32},{64,80},{80,64},{96,112},{112,96},{1... | collective-permute-start | bytes 960008 | tf_op jit(solution)/shard_map/ppermute | solution.py:41
  150.0 2.1 %collective-permute-start.40 = (bf16[100,1600]{1,0:T(8,128)(2,1)}, bf16[100,1600]{1,0:T(8,128)(2,1)}, u32[]{:S(2)}, u32[]{:S(2)}) collective-permute-start(bf16[100,1600]{1,0:T(8,128)(2,1)} %collective-permute-done.32.refs_3_), channel_id=1, source_target_pairs={{0,16},{16,0},{32,48},{48,32},{64,80},{80,64},{96,112},{112,96},{1... | collective-permute-start | bytes 960008 | tf_op jit(solution)/shard_map/ppermute | solution.py:41
  152.1 0.9 copy-start.4
  166.6 8.8 %collective-permute-start.43 = (bf16[100,200]{1,0:T(8,128)(2,1)S(1)}, bf16[100,200]{1,0:T(8,128)(2,1)S(1)}, u32[]{:S(2)}, u32[]{:S(2)}) collective-permute-start(bf16[100,200]{1,0:T(8,128)(2,1)S(1)} %taylor.1), channel_id=1, source_target_pairs={{0,0},{1,1},{2,2},{3,3},{4,16},{5,17},{6,18},{7,19},{8,32},{9,33},... | collective-permute-start | bytes 120008 | tf_op jit(solution)/shard_map/ppermute | solution.py:62
